TPU v7x, 32 devices: a whole 2x2x4 slice. The times are simulated.
32 devices in a mesh: dp: 16 (over z, y, x), fsdp: 2 (over core).
Axes of the slice: x: 2, y: 2, z: 4, core: 2. Of those that a mesh axis runs over, the one named last changes fastest.
Arguments:
- tokens: bfloat16 [64, 196, 512], P(('dp', 'fsdp')), may hold values from -6 to 6
- regions: int32 [196], replicated, may hold values from 0 to 3
- rel_index: int32 [2401], replicated, may hold values from 0 to 168
- norm_gains: bfloat16 [2, 2, 512], P(None, None, 'fsdp'), may hold values from 0.5 to 1.5
- norm_shifts: bfloat16 [2, 2, 512], P(None, None, 'fsdp'), may hold values from -1.75 to 1.75
- qkv_weight: bfloat16 [2, 512, 1536], P(None, 'fsdp'), may hold values from -0.25 to 0.25
- qv_bias: bfloat16 [2, 2, 512], P(None, None, 'fsdp'), may hold values from -1.75 to 1.75
- rel_table: bfloat16 [2, 169, 16], P(None, None, 'fsdp'), may hold values from -6 to 6
- proj_weight: bfloat16 [2, 512, 512], P(None, 'fsdp'), may hold values from -0.75 to 0.75
- proj_bias: bfloat16 [2, 512], P(None, 'fsdp'), may hold values from -1.75 to 1.75
- fc1_weight: bfloat16 [2, 512, 2048], P(None, 'fsdp'), may hold values from -0.25 to 0.25
- fc1_bias: bfloat16 [2, 2048], P(None, 'fsdp'), may hold values from -1.75 to 1.75
- fc2_weight: bfloat16 [2, 2048, 512], P(None, 'fsdp'), may hold values from -0.1875 to 0.1875
- fc2_bias: bfloat16 [2, 512], P(None, 'fsdp'), may hold values from -1.75 to 1.75
- cotangent: bfloat16 [64, 196, 512], P(('dp', 'fsdp')), may hold values from -6 to 6
Outputs:
- output: bfloat16 [64, 196, 512], P(('dp', 'fsdp'))
- tokens_grad: float32 [64, 196, 512], P(('dp', 'fsdp'))
- norm_gains_grad: float32 [2, 2, 512], P(None, None, 'fsdp')
- norm_shifts_grad: float32 [2, 2, 512], P(None, None, 'fsdp')
- qkv_weight_grad: float32 [2, 512, 1536], P(None, 'fsdp')
- qv_bias_grad: float32 [2, 2, 512], P(None, None, 'fsdp')
- rel_table_grad: float32 [2, 169, 16], P(None, None, 'fsdp')
- proj_weight_grad: float32 [2, 512, 512], P(None, 'fsdp')
- proj_bias_grad: float32 [2, 512], P(None, 'fsdp')
- fc1_weight_grad: float32 [2, 512, 2048], P(None, 'fsdp')
- fc1_bias_grad: float32 [2, 2048], P(None, 'fsdp')
- fc2_weight_grad: float32 [2, 2048, 512], P(None, 'fsdp')
- fc2_bias_grad: float32 [2, 512], P(None, 'fsdp')
All inputs are finite; a program needn't handle non-finite values.
Results may differ from a plain program's by a relative error of at most 0.018.
Values may be sent and summed in bfloat16 or wider, within the bound.
No kernel may reach another device: no remote copies, remote signals or barrier semaphores. Data moves between devices by JAX's collectives and lax.ppermute only.
A program may use at most 192 MiB of HBM per device.

v0:
```python
import functools

import numpy as np

import jax
import jax.numpy as jnp
from jax import lax
from jax.experimental import pallas as pl
from jax.experimental.pallas import tpu as pltpu
from jax.sharding import PartitionSpec as P

D = 512
HEADS = 16
HD = 32
FF = 2048
WIN = 7
IMG = 14
SHIFT = 3
PIX = 196
WT = 49
RELS = 169
ROWS = 64
CELL = 256
QUADS = 4
TIE = 0
LIVE = 176

norm_eps = 1e-05
scale = HD**-0.5
f32 = jnp.float32
bf16 = jnp.bfloat16


def place(offset):
    rows = np.full((CELL,), -1, np.int64)
    for i in range(IMG):
        for j in range(IMG):
            window = (i // WIN) * 2 + j // WIN
            row = window * ROWS + (i % WIN) * WIN + j % WIN
            rows[row] = ((i + offset) % IMG) * IMG + (j + offset) % IMG
    return rows


def permutations():
    base, moved = place(0), place(SHIFT)
    lay = np.zeros((CELL, PIX), np.float32)
    lay[base >= 0, base[base >= 0]] = 1
    shifted = np.zeros((CELL, PIX), np.float32)
    shifted[moved >= 0, moved[moved >= 0]] = 1
    return lay, lay.T.copy(), shifted @ lay.T, lay @ shifted.T


def dot(a, b):
    return jnp.dot(a, b, preferred_element_type=f32)


def dot_nt(a, b):
    return lax.dot_general(a, b, (((1,), (1,)), ((), ())), preferred_element_type=f32)


def dot_tn(a, b):
    return lax.dot_general(a, b, (((0,), (0,)), ((), ())), preferred_element_type=f32)


def loop(count, step):
    def run(at, carry):
        step(at)
        return carry

    lax.fori_loop(0, count, run, 0)


def span(at, size):
    return pl.ds(pl.multiple_of(at * size, size), size)


def normal(values):
    centred = values - jnp.mean(values, -1, keepdims=True)
    spread = lax.rsqrt(jnp.mean(centred * centred, -1, keepdims=True) + norm_eps)
    return centred * spread, spread


def norm_rows(source, target, gain, shift, rows):
    def step(at):
        part = span(at, 128)
        unit, _ = normal(source[part, :])
        target[part, :] = (unit * gain + shift).astype(bf16)

    loop(rows // 128, step)


def norm_back(grad, source, gain, extra, target, rows):
    def step(at, sums):
        part = span(at, 128)
        dh = grad[part, :]
        unit, spread = normal(source[part, :])
        du = dh * gain
        back = spread * (
            du
            - jnp.mean(du, -1, keepdims=True)
            - unit * jnp.mean(du * unit, -1, keepdims=True)
        )
        target[part, :] = extra[part, :] + back
        return (
            sums[0] + jnp.sum(dh * unit, 0, keepdims=True),
            sums[1] + jnp.sum(dh, 0, keepdims=True),
        )

    zero = jnp.zeros((1, D), f32)
    return lax.fori_loop(0, rows // 128, step, (zero, zero))


def move(matrix, source, target, rows, columns):
    for image in range(rows // CELL):
        for at in range(columns // D):
            target[image * CELL : (image + 1) * CELL, at * D : (at + 1) * D] = dot(
                matrix, source[image * CELL : (image + 1) * CELL, at * D : (at + 1) * D]
            ).astype(bf16)


def fetch(core, layer, own, other, target, sems):
    half = own.shape[1]
    mine = pltpu.make_async_copy(
        own.at[layer], target.at[pl.ds(pl.multiple_of(core * half, half), half), :], sems.at[0]
    )
    theirs = pltpu.make_async_copy(
        other.at[layer],
        target.at[pl.ds(pl.multiple_of((1 - core) * half, half), half), :],
        sems.at[1],
    )
    mine.start()
    theirs.start()

    def wait():
        mine.wait()
        theirs.wait()

    return wait


def give(core, grads, keep, send, sems):
    one = pltpu.make_async_copy(grads.at[core], keep, sems.at[0])
    two = pltpu.make_async_copy(grads.at[1 - core], send, sems.at[1])
    one.start()
    two.start()
    one.wait()
    two.wait()


def head_masks():
    lanes = lax.broadcasted_iota(jnp.int32, (ROWS, 128), 1) // HD
    return [lanes == at for at in range(QUADS)]


def stack_heads(value, masks):
    zero = jnp.zeros_like(value)
    return jnp.concatenate([jnp.where(mask, value, zero) for mask in masks], axis=0)


def pick_heads(value, masks):
    result = value[:ROWS]
    for at in range(1, QUADS):
        result = jnp.where(masks[at], value[at * ROWS : (at + 1) * ROWS], result)
    return result


def attention_forward_kernel(
    layer,
    rows,
    core_ref,
    source,
    lay,
    to_moved,
    from_moved,
    small,
    bias,
    mask,
    qkv_own,
    qkv_other,
    proj_own,
    proj_other,
    middle,
    normed,
    qkv,
    probs,
    mixed,
    qkv_w,
    proj_w,
    tokens_in,
    work,
    sems,
):
    core = core_ref[0]
    wait_qkv = fetch(core, layer, qkv_own, qkv_other, qkv_w, sems.at[0])
    wait_proj = fetch(core, layer, proj_own, proj_other, proj_w, sems.at[1])
    if layer == 0:
        for image in range(rows // CELL):
            tokens_in[image * CELL : (image + 1) * CELL, :] = dot(lay[...], source[image])
    else:
        tokens_in = source
    norm_rows(tokens_in, normed, small[0:1, :], small[2:3, :], rows)
    if layer == 0:
        moved = normed
    else:
        move(to_moved[...], normed, work, rows, D)
        moved = work
    wait_qkv()
    for at in range(3):
        part = dot(moved[...], qkv_w[:, at * D : (at + 1) * D])
        if at == 0:
            part = part + small[4:5, :]
        if at == 2:
            part = part + small[5:6, :]
        qkv[:, at * D : (at + 1) * D] = part.astype(bf16)
    masks = head_masks()
    out = mixed if layer == 0 else work

    def window(at):
        part = span(at, ROWS)
        for quad in range(QUADS):
            lanes = slice(quad * 128, (quad + 1) * 128)
            queries = stack_heads(qkv[part, lanes], masks)
            keys = qkv[part, D + quad * 128 : D + (quad + 1) * 128]
            values = qkv[part, 2 * D + quad * 128 : 2 * D + (quad + 1) * 128]
            scores = scale * dot_nt(keys, queries) + bias[quad]
            if layer:
                scores = scores + mask[at % 4]
            expo = jnp.exp(scores - jnp.max(scores, 0, keepdims=True))
            prob = expo / jnp.sum(expo, 0, keepdims=True)
            probs[at, quad] = prob
            mix = dot_tn(prob.astype(bf16), values)
            out[part, lanes] = pick_heads(mix, masks).astype(bf16)

    loop(rows // ROWS, window)
    if layer:
        move(from_moved[...], work, mixed, rows, D)
    wait_proj()
    middle[...] = tokens_in[...] + dot(mixed[...], proj_w[...]) + small[6:7, :]


def mlp_forward_kernel(
    layer,
    rows,
    core_ref,
    middle,
    small,
    up_own,
    up_other,
    down_own,
    down_other,
    result,
    normed,
    hidden,
    slope,
    up_w,
    down_w,
    sems,
):
    core = core_ref[0]
    wait_up = fetch(core, layer, up_own, up_other, up_w, sems.at[0])
    wait_down = fetch(core, layer, down_own, down_other, down_w, sems.at[1])
    norm_rows(middle, normed, small[1:2, :], small[3:4, :], rows)
    wait_up()

    def step(at):
        part = span(at, 256)
        inner = dot(normed[...], up_w[:, part])
        row = 8 + at // 2
        inner = inner + small[pl.ds(row, 1), span(at % 2, 256)]
        below = 0.5 * (1.0 + lax.erf(inner * (0.5**0.5)))
        hidden[:, part] = (inner * below).astype(bf16)
        slope[:, part] = (
            below + inner * (jnp.exp(-0.5 * inner * inner) * ((2 * np.pi) ** -0.5))
        ).astype(bf16)

    loop(FF // 256, step)
    wait_down()
    result[...] = (
        middle[...] + dot(hidden[...], down_w[...]) + small[7:8, :]
    ).astype(result.dtype)


def mlp_backward_kernel(
    layer,
    rows,
    core_ref,
    grad,
    lay,
    middle,
    normed,
    hidden,
    slope,
    small,
    up_own,
    up_other,
    down_own,
    down_other,
    middle_grad,
    sums,
    keep,
    send,
    up_w,
    down_w,
    grads,
    inner_grad,
    grad_in,
    low,
    turned,
    normed_grad,
    sems,
):
    core = core_ref[0]
    wait_up = fetch(core, layer, up_own, up_other, up_w, sems.at[0])
    wait_down = fetch(core, layer, down_own, down_other, down_w, sems.at[1])
    if layer == 1:
        for image in range(rows // CELL):
            grad_in[image * CELL : (image + 1) * CELL, :] = dot(lay[...], grad[image])
    else:
        grad_in = grad
    low[...] = grad_in[...].astype(bf16)
    sums[...] = jnp.zeros(sums.shape, f32)
    sums[2:3, :] = jnp.sum(low[...].astype(f32), 0, keepdims=True)
    turned[...] = normed[...].T
    wait_down()

    def step(at):
        part = span(at, 256)
        back = dot_nt(low[...], down_w[part, :]) * slope[:, part].astype(f32)
        back = back.astype(bf16)
        inner_grad[:, part] = back
        sums[pl.ds(3 + at // 2, 1), span(at % 2, 256)] = jnp.sum(
            back.astype(f32), 0, keepdims=True
        )
        down_grad = dot(hidden[:, part].T, low[...]).astype(bf16)
        grads[at // 4, pl.ds(pl.multiple_of(1024 + (at % 4) * 256, 256), 256), :] = down_grad
        up_grad = dot(turned[...], back).astype(bf16)
        place_at = pl.ds(pl.multiple_of((at // 2) * 256, 256), 256)
        lanes = span(at % 2, 256)
        grads[0, place_at, lanes] = up_grad[:256]
        grads[1, place_at, lanes] = up_grad[256:]

    loop(FF // 256, step)
    wait_up()
    normed_grad[...] = dot_nt(inner_grad[...], up_w[...])
    gain_sum, shift_sum = norm_back(normed_grad, middle, small[1:2, :], grad_in, middle_grad, rows)
    sums[0:1, :] = gain_sum
    sums[1:2, :] = shift_sum
    give(core, grads, keep, send, sems.at[2])


def attention_backward_kernel(
    layer,
    rows,
    core_ref,
    middle_grad,
    source,
    lay,
    unlay,
    to_moved,
    from_moved,
    normed,
    qkv,
    probs,
    mixed,
    small,
    qkv_own,
    qkv_other,
    proj_own,
    proj_other,
    source_grad,
    sums,
    pairs,
    keep,
    send,
    qkv_w,
    proj_w,
    grads,
    tokens_in,
    low,
    mix_grad,
    joined,
    moved_grad,
    turned,
    normed_grad,
    sems,
):
    core = core_ref[0]
    wait_qkv = fetch(core, layer, qkv_own, qkv_other, qkv_w, sems.at[0])
    wait_proj = fetch(core, layer, proj_own, proj_other, proj_w, sems.at[1])
    if layer == 0:
        for image in range(rows // CELL):
            tokens_in[image * CELL : (image + 1) * CELL, :] = dot(lay[...], source[image])
    else:
        tokens_in = source
    low[...] = middle_grad[...].astype(bf16)
    sums[...] = jnp.zeros(sums.shape, f32)
    sums[4:5, :] = jnp.sum(low[...].astype(f32), 0, keepdims=True)
    turned[...] = mixed[...].T
    for side in range(2):
        grads[side, 768:1024, :] = dot(turned[side * 256 : (side + 1) * 256, :], low[...]).astype(
            bf16
        )
    wait_proj()
    if layer == 0:
        mix_grad[...] = dot_nt(low[...], proj_w[...]).astype(bf16)
        target = joined
    else:
        moved_grad[:, :D] = dot_nt(low[...], proj_w[...]).astype(bf16)
        move(to_moved[...], moved_grad, mix_grad, rows, D)
        target = moved_grad
    pairs[...] = jnp.zeros(pairs.shape, f32)
    masks = head_masks()

    def window(at):
        part = span(at, ROWS)
        for quad in range(QUADS):
            queries = stack_heads(qkv[part, quad * 128 : (quad + 1) * 128], masks)
            keys = qkv[part, D + quad * 128 : D + (quad + 1) * 128]
            values = qkv[part, 2 * D + quad * 128 : 2 * D + (quad + 1) * 128]
            given = stack_heads(mix_grad[part, quad * 128 : (quad + 1) * 128], masks)
            prob = probs[at, quad]
            prob_grad = dot_nt(values, given)
            delta = jnp.sum(prob_grad * prob, 0, keepdims=True)
            score_grad = (prob * (prob_grad - delta)).astype(bf16)
            pairs[quad] += score_grad.astype(f32)
            values_grad = dot(prob.astype(bf16), given)
            keys_grad = scale * dot(score_grad, queries)
            queries_grad = scale * pick_heads(dot_tn(score_grad, keys), masks)
            target[part, quad * 128 : (quad + 1) * 128] = queries_grad.astype(bf16)
            target[part, D + quad * 128 : D + (quad + 1) * 128] = keys_grad.astype(bf16)
            target[part, 2 * D + quad * 128 : 2 * D + (quad + 1) * 128] = values_grad.astype(bf16)

    loop(rows // ROWS, window)
    if layer:
        move(from_moved[...], moved_grad, joined, rows, 3 * D)
    sums[2:3, :] = jnp.sum(joined[:, :D].astype(f32), 0, keepdims=True)
    sums[3:4, :] = jnp.sum(joined[:, 2 * D :].astype(f32), 0, keepdims=True)
    turned[...] = normed[...].T
    for at in range(3):
        for side in range(2):
            grads[side, at * 256 : (at + 1) * 256, :] = dot(
                turned[side * 256 : (side + 1) * 256, :], joined[:, at * D : (at + 1) * D]
            ).astype(bf16)
    wait_qkv()
    normed_grad[...] = dot_nt(joined[...], qkv_w[...])
    if layer == 0:
        gain_sum, shift_sum = norm_back(
            normed_grad, tokens_in, small[0:1, :], middle_grad, normed_grad, rows
        )
        for image in range(rows // CELL):
            value = normed_grad[image * CELL : (image + 1) * CELL, :]
            high = value.astype(bf16)
            rest = value - high.astype(f32)
            fine = rest.astype(bf16)
            last = (rest - fine.astype(f32)).astype(bf16)
            source_grad[image] = (
                dot(unlay[...], high) + dot(unlay[...], fine) + dot(unlay[...], last)
            )
    else:
        gain_sum, shift_sum = norm_back(
            normed_grad, tokens_in, small[0:1, :], middle_grad, source_grad, rows
        )
    sums[0:1, :] = gain_sum
    sums[1:2, :] = shift_sum
    give(core, grads, keep, send, sems.at[2])


def call(kernel, layer, rows, core, inputs, kinds, outs, out_kinds, scratch, flops):
    spaces = {"v": pltpu.VMEM, "a": pl.ANY}
    return pl.pallas_call(
        functools.partial(kernel, layer, rows),
        in_specs=[pl.BlockSpec(memory_space=pltpu.SMEM)]
        + [pl.BlockSpec(memory_space=spaces[kind]) for kind in kinds],
        out_specs=[pl.BlockSpec(memory_space=spaces[kind]) for kind in out_kinds],
        out_shape=outs,
        scratch_shapes=scratch,
        compiler_params=pltpu.CompilerParams(vmem_limit_bytes=56 * 1024 * 1024),
        cost_estimate=pl.CostEstimate(flops=1, bytes_accessed=1, transcendentals=0),
        name=kernel.__name__ + str(layer),
    )(core, *inputs)


def shape(dims, dtype):
    return jax.ShapeDtypeStruct(dims, dtype)


def swap_cores(value):
    return lax.ppermute(value, "fsdp", [(0, 1), (1, 0)])


def in_order(own, other, axis):
    first = lax.axis_index("fsdp") == 0
    return jnp.concatenate([jnp.where(first, own, other), jnp.where(first, other, own)], axis=axis)


def dp_swap(value, bit, count):
    return lax.ppermute(value, "dp", [(at, at ^ (1 << bit)) for at in range(count)])


def plus(one, two):
    return (one.astype(f32) + two.astype(f32)).astype(bf16)


def op_first(bits, ins, outs):
    quarter = outs[0].shape[0] // 2
    for part in range(2):
        keep, got = ins[2 * part : 2 * part + 2]
        send, hold = outs[2 * part : 2 * part + 2]
        side = bits[part]
        for low in range(2):
            rows = slice(low * quarter, (low + 1) * quarter)
            send[rows, :] = plus(keep[2 * (1 - side) + low], got[2 * (1 - side) + low])
            hold[rows, :] = plus(keep[2 * side + low], got[2 * side + low])


def op_first_small(bits, ins, outs):
    quarter = outs[0].shape[0] // 2
    rows_in = quarter - 16
    tiny, tiny_got = ins[4:6]
    for part in range(2):
        keep, got = ins[2 * part : 2 * part + 2]
        send, hold = outs[2 * part : 2 * part + 2]
        side = bits[part]
        for low in range(2):
            first = slice(low * quarter, low * quarter + rows_in)
            last = slice(low * quarter + rows_in, (low + 1) * quarter)
            for target, at in ((send, 2 * (1 - side) + low), (hold, 2 * side + low)):
                target[first, :] = plus(keep[at], got[at])
                target[last, :] = plus(tiny[4 * part + at], tiny_got[4 * part + at])


def op_second(bits, ins, outs):
    for part in range(2):
        hold, got = ins[2 * part : 2 * part + 2]
        send, rest = outs[2 * part : 2 * part + 2]
        side = bits[1 - part]
        send[...] = plus(hold[1 - side], got[1 - side])
        rest[...] = plus(hold[side], got[side])


def op_join(bits, ins, outs):
    quarter = ins[0].shape[0]
    for part in range(2):
        outs[0][part * quarter : (part + 1) * quarter, :] = plus(
            ins[2 * part][...], ins[2 * part + 1][...]
        )


def op_add(bits, ins, outs):
    outs[0][...] = plus(ins[0][...], ins[1][...])


def step_kernel(plan, bits_ref, *refs):
    bits = (bits_ref[0], bits_ref[1])
    total = sum(item[1] for item in plan)
    ins, outs = refs[:total], refs[total:]
    for op, inputs, outputs in plan:
        op(bits, ins[:inputs], outs[:outputs])
        ins, outs = ins[inputs:], outs[outputs:]


class Group:
    def __init__(self, rows, parts, count, tiny=None):
        self.small = tiny
        self.quarter = rows // 4 + (16 if tiny else 0)
        self.parts = parts
        self.count = count
        self.stage = 0
        self.later = count.bit_length() - 3
        self.done = False

    def low(self, rows):
        return shape((rows, D), bf16)

    def next_op(self):
        q = self.quarter
        if self.stage == 0:
            ins = [item.reshape(4, -1, D) for pair in self.parts for item in pair]
            if self.small:
                ins += [item.reshape(8, 16, D) for item in self.small]
            return op_first_small if self.small else op_first, ins, [self.low(2 * q)] * 4
        if self.stage == 1:
            ins = [item.reshape(2, q, D) for item in self.state]
            return op_second, ins, [self.low(q)] * 4
        if self.stage == 2:
            return op_join, self.state, [self.low(2 * q)]
        if self.stage < 3 + self.later:
            return op_add, self.state, [self.low(2 * q)]
        return None

    def send(self, outs):
        if self.stage < 2:
            first, second = (0, 1) if self.stage == 0 else (1, 0)
            self.state = [
                outs[1],
                dp_swap(outs[0], first, self.count),
                outs[3],
                dp_swap(outs[2], second, self.count),
            ]
        elif self.stage < 2 + self.later:
            self.state = [outs[0], dp_swap(outs[0], self.stage, self.count)]
        elif self.stage == 2 + self.later:
            mine = outs[0]
            self.state = [mine, dp_swap(mine, 0, self.count), dp_swap(mine, 1, self.count)]
        else:
            q = self.quarter
            mine, by_x, by_y = self.state
            self.state = [
                mine,
                by_x,
                by_y,
                dp_swap(by_x[:q], 1, self.count),
                dp_swap(by_y[q:], 0, self.count),
            ]
            self.done = True
        self.stage += 1


def after(first, then):
    return lax.optimization_barrier((first, then))[1]


def advance(groups, bits, when, final=False):
    ops, marks = [], []
    for group in groups:
        op = group.next_op()
        if op is None:
            group.state = list(after(when, group.state))
            group.send(None)
        else:
            ops.append((group, op))
    if not ops:
        return when
    plan = tuple((op[0], len(op[1]), len(op[2])) for _, op in ops)
    inputs = [item for _, op in ops for item in op[1]]
    outs = [item for _, op in ops for item in op[2]]
    inputs = after(when, inputs)
    results = pl.pallas_call(
        functools.partial(step_kernel, plan),
        in_specs=[pl.BlockSpec(memory_space=pltpu.SMEM)]
        + [pl.BlockSpec(memory_space=pltpu.VMEM)] * len(inputs),
        out_specs=[pl.BlockSpec(memory_space=pltpu.VMEM)] * len(outs),
        out_shape=outs,
        compiler_params=pltpu.CompilerParams(vmem_limit_bytes=56 * 1024 * 1024),
        cost_estimate=pl.CostEstimate(flops=1, bytes_accessed=1, transcendentals=0),
        name="reduce_step",
    )(bits, *inputs)
    for group, op in ops:
        mine, results = results[: len(op[2])], results[len(op[2]) :]
        group.send(mine)
        marks.append(mine[0])
    return marks[0]


def merge_kernel(*refs):
    out = refs[-1]
    start = 0
    for at in range(0, len(refs) - 1, 2):
        rows = refs[at].shape[0]
        out[start : start + rows, :] = plus(refs[at][...], refs[at + 1][...])
        start += rows


def quarters(ins, x, y, target):
    mine, by_x, by_y, far_first, far_second = ins
    q = far_first.shape[0]
    target[x * 2 + y] = mine[:q, :]
    target[(1 - x) * 2 + y] = by_x[:q, :]
    target[x * 2 + 1 - y] = by_y[:q, :]
    target[(1 - x) * 2 + 1 - y] = far_first[...]
    target[4 + y * 2 + x] = mine[q:, :]
    target[4 + y * 2 + 1 - x] = by_x[q:, :]
    target[4 + (1 - y) * 2 + x] = by_y[q:, :]
    target[4 + (1 - y) * 2 + 1 - x] = far_second[...]


def unpack_kernel(bits_ref, *refs):
    x, y, core = bits_ref[0], bits_ref[1], bits_ref[2]
    mlp_in, attn_in, upper = refs[:5], refs[5:10], refs[10]
    qkv_out, proj_out, up_out, down_out = refs[11:15]
    gains_out, shifts_out, qv_out, proj_b_out, up_b_out, down_b_out, table_out = refs[15:22]
    mlp, attn, tiny = refs[22:]
    half = D // 2
    for at in range(2):
        up_out[1, :, 2 * at * D : (2 * at + 1) * D] = upper[2 * at * half : (2 * at + 1) * half, :].astype(f32)
        up_out[1, :, (2 * at + 1) * D : (2 * at + 2) * D] = upper[
            (2 * at + 1) * half : (2 * at + 2) * half, :
        ].astype(f32)
    down_out[1] = upper[2 * D : 4 * D, :].astype(f32)
    for at in range(3):
        qkv_out[1, :, at * D : (at + 1) * D] = upper[
            4 * D + at * half : 4 * D + (at + 1) * half, :
        ].astype(f32)
    proj_out[1] = upper[4 * D + 3 * half : 6 * D, :].astype(f32)
    tiny[1] = upper[6 * D :, :].astype(f32)
    quarters(mlp_in, x, y, mlp)
    quarters(attn_in, x, y, attn)
    for at in range(4):
        up_out[0, :, at * D : (at + 1) * D] = mlp[at].astype(f32)
        down_out[0, at * half : (at + 1) * half, :] = mlp[4 + at].astype(f32)
    q = half // 2
    for at in range(8):
        rows = slice((at % 2) * q, (at % 2 + 1) * q)
        value = attn[at, :q, :].astype(f32)
        if at < 6:
            qkv_out[0, rows, (at // 2) * D : (at // 2 + 1) * D] = value
        else:
            proj_out[0, rows, :] = value
    for at in range(2):
        tiny[0, at * 16 : (at + 1) * 16, :] = attn[at, q : q + 16, :].astype(f32)
    first = core == 0

    def own(row):
        return jnp.where(first, row[:, :half], row[:, half:])

    for layer in range(2):
        sums = tiny[layer]
        for norm in range(2):
            gains_out[layer, norm : norm + 1, :] = own(sums[8 * norm : 8 * norm + 1])
            shifts_out[layer, norm : norm + 1, :] = own(sums[8 * norm + 1 : 8 * norm + 2])
            qv_out[layer, norm : norm + 1, :] = own(sums[2 + norm : 3 + norm])
            up_b_out[layer : layer + 1, norm * D : (norm + 1) * D] = jnp.where(
                first, sums[11 + norm : 12 + norm], sums[13 + norm : 14 + norm]
            )
        proj_b_out[layer : layer + 1, :] = own(sums[4:5])
        down_b_out[layer : layer + 1, :] = own(sums[10:11])
        table_out[layer] = jnp.where(first, sums[16:24, :256], sums[24:32, :256])


def body(
    tokens,
    regions,
    rel_index,
    norm_gains,
    norm_shifts,
    qkv_weight,
    qv_bias,
    rel_table,
    proj_weight,
    proj_bias,
    fc1_weight,
    fc1_bias,
    fc2_weight,
    fc2_bias,
    cotangent,
):
    count = lax.axis_size("dp")
    images = tokens.shape[0]
    rows = images * CELL
    windows = images * 4
    own_small = jnp.concatenate(
        [
            norm_gains,
            norm_shifts,
            qv_bias,
            proj_bias[:, None],
            fc2_bias[:, None],
            fc1_bias.reshape(2, 4, D // 2),
        ],
        axis=1,
    )
    own_table = rel_table
    qkv_other = swap_cores(qkv_weight)
    proj_other = swap_cores(proj_weight)
    other_small = swap_cores(own_small)
    other_table = swap_cores(own_table)
    up_other = swap_cores(fc1_weight)
    down_other = swap_cores(fc2_weight)

    core = lax.axis_index("fsdp").astype(jnp.int32).reshape(1)
    eight = in_order(own_small[:, :8], other_small[:, :8], 2)
    four = in_order(
        own_small[:, 8:].reshape(2, 2, D), other_small[:, 8:].reshape(2, 2, D), 1
    )
    small_all = jnp.concatenate([eight, four, jnp.zeros((2, 4, D), bf16)], axis=1).astype(f32)
    table = in_order(own_table, other_table, 2)
    table = jnp.concatenate(
        [table, jnp.full((2, 1, HEADS), -1e30, bf16), jnp.zeros((2, LIVE - RELS - 1, HEADS), bf16)],
        axis=1,
    )
    grid_index = rel_index.reshape(WT, WT).T
    grid_index = jnp.pad(grid_index, ((0, 0), (0, ROWS - WT)))
    grid_index = jnp.pad(grid_index, ((0, ROWS - WT), (0, 0)), constant_values=RELS)
    onehot = (
        grid_index.reshape(1, ROWS * ROWS) == jnp.arange(LIVE, dtype=jnp.int32)[:, None]
    ).astype(bf16)
    bias_all = jnp.einsum("lrh,rp->lhp", table, onehot, preferred_element_type=f32)
    bias_all = (
        bias_all.reshape(2, QUADS, 4, ROWS, ROWS)
        .transpose(0, 1, 3, 2, 4)
        .reshape(2, QUADS, ROWS, 4 * ROWS)
    )
    region_win = (
        regions.reshape(2, WIN, 2, WIN).transpose(0, 2, 1, 3).reshape(4, WT)
    )
    mask = jnp.where(region_win[:, :, None] == region_win[:, None, :], 0.0, -100.0).astype(f32)
    mask = jnp.pad(mask, ((0, 0), (0, ROWS - WT), (0, ROWS - WT)))
    mask = jnp.tile(mask, (1, 1, 4))
    lay, unlay, to_moved, from_moved = [jnp.asarray(item, bf16) for item in permutations()]

    vmem = pltpu.VMEM
    wide = (rows, D)
    attn_w = [vmem((D, 3 * D), bf16), vmem((D, D), bf16)]
    mlp_w = [vmem((D, FF), bf16), vmem((FF, D), bf16)]
    two_sems = pltpu.SemaphoreType.DMA((2, 2))
    three_sems = pltpu.SemaphoreType.DMA((3, 2))
    attn_flops = 2 * rows * D * D * 5
    mlp_flops = 2 * rows * D * FF * 2
    current = tokens
    saved = []
    for layer in range(2):
        small = small_all[layer]
        middle, normed, qkv, probs, mixed = call(
            attention_forward_kernel,
            layer,
            rows,
            core,
            [
                current,
                lay,
                to_moved,
                from_moved,
                small,
                bias_all[layer],
                mask,
                qkv_weight,
                qkv_other,
                proj_weight,
                proj_other,
            ],
            "vvvvvvvaaaa",
            [
                shape(wide, f32),
                shape(wide, bf16),
                shape((rows, 3 * D), bf16),
                shape((windows, QUADS, ROWS, 4 * ROWS), f32),
                shape(wide, bf16),
            ],
            "vvvvv",
            attn_w + [vmem(wide if layer == 0 else (8, 128), f32), vmem(wide, bf16), two_sems],
            attn_flops,
        )
        result, normed_two, hidden, slope = call(
            mlp_forward_kernel,
            layer,
            rows,
            core,
            [middle, small, fc1_weight, up_other, fc2_weight, down_other],
            "vvaaaa",
            [
                shape(wide, f32),
                shape(wide, bf16),
                shape((rows, FF), bf16),
                shape((rows, FF), bf16),
            ],
            "vvvv",
            mlp_w + [two_sems],
            mlp_flops,
        )
        saved.append((current, middle, normed, qkv, probs, mixed, normed_two, hidden, slope, small))
        current = result
    at_dp = lax.axis_index("dp")
    bits = jnp.stack([at_dp & 1, (at_dp >> 1) & 1, lax.axis_index("fsdp")]).astype(jnp.int32)
    onehot_f = onehot.astype(f32)

    def small_rows(attn_sums, mlp_sums, pairs):
        flat = pairs.reshape(QUADS, ROWS, 4, ROWS).transpose(0, 2, 1, 3).reshape(HEADS, -1)
        heads = jnp.einsum("hp,rp->hr", flat, onehot_f, precision=lax.Precision.HIGHEST)
        heads = jnp.pad(heads, ((0, 0), (0, D - LIVE)))
        return jnp.concatenate([attn_sums, mlp_sums, heads], axis=0).astype(bf16)

    def backward(layer, grad, kept):
        source, middle, normed, qkv, probs, mixed, normed_two, hidden, slope, small = kept
        middle_grad, mlp_sums, mlp_keep, mlp_send = call(
            mlp_backward_kernel,
            layer,
            rows,
            core,
            [
                grad,
                lay,
                middle,
                normed_two,
                hidden,
                slope,
                small,
                fc1_weight,
                up_other,
                fc2_weight,
                down_other,
            ],
            "vvvvvvvaaaa",
            [
                shape(wide, f32),
                shape((8, D), f32),
                shape((FF, D), bf16),
                shape((FF, D), bf16),
            ],
            "vvaa",
            mlp_w
            + [
                vmem((2, FF, D), bf16),
                vmem((rows, FF), bf16),
                vmem(wide if layer == 1 else (8, 128), f32),
                vmem(wide, bf16),
                vmem((D, rows), bf16),
                vmem(wide, f32),
                three_sems,
            ],
            2 * mlp_flops,
        )
        mlp_got = swap_cores(mlp_send)
        if layer == 0:
            mlp_group = Group(2 * D, [
                (mlp_keep[: 2 * D], mlp_got[: 2 * D]),
                (mlp_keep[2 * D :], mlp_got[2 * D :]),
            ], count)
            mark = advance([mlp_group], bits, mlp_sums)
            middle_grad = after(mark, middle_grad)
        grad, attn_sums, pairs, attn_keep, attn_send = call(
            attention_backward_kernel,
            layer,
            rows,
            core,
            [
                middle_grad,
                source,
                lay,
                unlay,
                to_moved,
                from_moved,
                normed,
                qkv,
                probs,
                mixed,
                small,
                qkv_weight,
                qkv_other,
                proj_weight,
                proj_other,
            ],
            "vvvvvvvvvvvaaaa",
            [
                shape(wide if layer else (images, PIX, D), f32),
                shape((8, D), f32),
                shape((QUADS, ROWS, 4 * ROWS), f32),
                shape((2 * D, D), bf16),
                shape((2 * D, D), bf16),
            ],
            "vvvaa",
            attn_w
            + [
                vmem((2, 2 * D, D), bf16),
                vmem(wide if layer == 0 else (8, 128), f32),
                vmem(wide, bf16),
                vmem(wide, bf16),
                vmem((rows, 3 * D), bf16),
                vmem((rows, 3 * D) if layer else (16, 128), bf16),
                vmem((D, rows), bf16),
                vmem(wide, f32),
                three_sems,
            ],
            2 * attn_flops,
        )
        if layer == 0:
            held = (grad, attn_sums, pairs, attn_keep, attn_send, mlp_group.state)
            grad, attn_sums, pairs, attn_keep, attn_send, mlp_group.state = (
                lax.optimization_barrier(held)
            )
        attn_got = swap_cores(attn_send)
        tiny = small_rows(attn_sums, mlp_sums, pairs)
        tiny_got = swap_cores(tiny)
        if layer == 1:
            upper = pl.pallas_call(
                merge_kernel,
                out_shape=shape((6 * D + 32, D), bf16),
                compiler_params=pltpu.CompilerParams(vmem_limit_bytes=56 * 1024 * 1024),
                name="merge",
            )(mlp_keep, mlp_got, attn_keep, attn_got, tiny, tiny_got)
            return lax.optimization_barrier((upper, grad))
        pad = ((0, 96), (0, 0))
        attn_group = Group(
            D,
            [(attn_keep[:D], attn_got[:D]), (attn_keep[D:], attn_got[D:])],
            count,
            (jnp.pad(tiny, pad), jnp.pad(tiny_got, pad)),
        )
        groups = [mlp_group, attn_group]
        mark = grad
        while not all(group.done for group in groups):
            mark = advance([group for group in groups if not group.done], bits, mark)
        return [grad] + mlp_group.state + attn_group.state

    upper, grad = backward(1, cotangent, saved[1])
    upper = lax.psum(upper, "dp")
    taken = (grad, saved[0])
    grad, *arrived = lax.cond(
        lax.optimization_barrier(jnp.bool_(True)),
        lambda taken: backward(0, *taken),
        lambda taken: [
            jnp.zeros(item.shape, item.dtype)
            for item in jax.eval_shape(lambda taken: backward(0, *taken), taken)
        ],
        taken,
    )
    output = lax.reduce_precision(current, 8, 7).astype(bf16)
    output = (
        output.reshape(images, 2, 2, ROWS, D)[:, :, :, :WT]
        .reshape(images, 2, 2, WIN, WIN, D)
        .transpose(0, 1, 3, 2, 4, 5)
        .reshape(images, PIX, D)
    )
    pieces = [*arrived, upper]
    (
        qkv_g, proj_g, up_g, down_g, gains_g, shifts_g, qv_g, proj_b_g, up_b_g, down_b_g, heads,
    ) = pl.pallas_call(
        unpack_kernel,
        in_specs=[pl.BlockSpec(memory_space=pltpu.SMEM)]
        + [pl.BlockSpec(memory_space=pltpu.VMEM)] * len(pieces),
        out_specs=[pl.BlockSpec(memory_space=pltpu.VMEM)] * 11,
        out_shape=[
            shape(item.shape, f32)
            for item in (
                qkv_weight,
                proj_weight,
                fc1_weight,
                fc2_weight,
                norm_gains,
                norm_shifts,
                qv_bias,
                proj_bias,
                fc1_bias,
                fc2_bias,
            )
        ]
        + [shape((2, HEADS // 2, 256), f32)],
        scratch_shapes=[
            vmem((8, D // 2, D), bf16),
            vmem((8, D // 4 + 16, D), bf16),
            vmem((2, 32, D), f32),
        ],
        compiler_params=pltpu.CompilerParams(vmem_limit_bytes=56 * 1024 * 1024),
        name="unpack",
    )(bits, *pieces)
    table_g = heads[:, :, :RELS].transpose(0, 2, 1)
    return (
        output,
        grad,
        gains_g,
        shifts_g,
        qkv_g,
        qv_g,
        table_g,
        proj_g,
        proj_b_g,
        up_g,
        up_b_g,
        down_g,
        down_b_g,
    )


def solution(mesh):
    return jax.shard_map(
        body,
        mesh=mesh,
        in_specs=(
            P(("dp", "fsdp"), None, None),
            P(),
            P(),
            P(None, None, "fsdp"),
            P(None, None, "fsdp"),
            P(None, "fsdp", None),
            P(None, None, "fsdp"),
            P(None, None, "fsdp"),
            P(None, "fsdp", None),
            P(None, "fsdp"),
            P(None, "fsdp", None),
            P(None, "fsdp"),
            P(None, "fsdp", None),
            P(None, "fsdp"),
            P(("dp", "fsdp"), None, None),
        ),
        out_specs=(
            P(("dp", "fsdp"), None, None),
            P(("dp", "fsdp"), None, None),
            P(None, None, "fsdp"),
            P(None, None, "fsdp"),
            P(None, "fsdp", None),
            P(None, None, "fsdp"),
            P(None, None, "fsdp"),
            P(None, "fsdp", None),
            P(None, "fsdp"),
            P(None, "fsdp", None),
            P(None, "fsdp"),
            P(None, "fsdp", None),
            P(None, "fsdp"),
        ),
        check_vma=False,
    )
```

profile of v0, /device:TPU:0, one launch (start us, length us, event | category | flops | bytes accessed | tf_op | source)
XLA Modules:
  0.0 338.8 jit_solution(7926074272471216983)
XLA Ops:
  34.7 11.9 %attention_forward_kernel0.1 = (f32[512,512]{1,0:T(8,128)S(1)}, bf16[512,512]{1,0:T(8,128)(2,1)}, bf16[512,1536]{1,0:T(8,128)(2,1)}, f32[8,4,64,256]{3,2,1,0:T(8,128)}, bf16[512,512]{1,0:T(8,128)(2,1)}) custom-call(s32[1]{0:T(128)} %bitcast.19.core_ref, bf16[2,196,512]{2,1,0:T(8,128)(2,1)} %copy.59.source, bf16[256,196]{1,0:T(8,128)(2,1)S(1)} %copy-done.11, ...), custom_call_target="tpu_custom_call" | custom-call | flops 1 | bytes 1 | tf_op jit(solution)/shard_map/attention_forward_kernel0/pallas_call | solution.py:470
  46.7 7.8 %mlp_forward_kernel0.1 = (f32[512,512]{1,0:T(8,128)}, bf16[512,512]{1,0:T(8,128)(2,1)}, bf16[512,2048]{1,0:T(8,128)(2,1)}, bf16[512,2048]{1,0:T(8,128)(2,1)}) custom-call(s32[1]{0:T(128)} %bitcast.19.core_ref, f32[512,512]{1,0:T(8,128)S(1)} %get-tuple-element.222.middle, f32[16,512]{1,0:T(8,128)S(1)} %get-tuple-element.402.small, ...), custom_call_target="tpu_custom_call" | custom-call | flops 1 | bytes 1 | tf_op jit(solution)/shard_map/mlp_forward_kernel0/pallas_call | solution.py:470
  54.5 12.3 %attention_forward_kernel1.1 = (f32[512,512]{1,0:T(8,128)}, bf16[512,512]{1,0:T(8,128)(2,1)}, bf16[512,1536]{1,0:T(8,128)(2,1)}, f32[8,4,64,256]{3,2,1,0:T(8,128)}, bf16[512,512]{1,0:T(8,128)(2,1)}) custom-call(s32[1]{0:T(128)} %bitcast.19.core_ref, f32[512,512]{1,0:T(8,128)} %get-tuple-element.223.source, bf16[256,196]{1,0:T(8,128)(2,1)S(1)} %copy-done.11, ...), custom_call_target="tpu_custom_call" | custom-call | flops 1 | bytes 1 | tf_op jit(solution)/shard_map/attention_forward_kernel1/pallas_call | solution.py:470
  66.9 8.6 %mlp_forward_kernel1.1 = (f32[512,512]{1,0:T(8,128)}, bf16[512,512]{1,0:T(8,128)(2,1)}, bf16[512,2048]{1,0:T(8,128)(2,1)}, bf16[512,2048]{1,0:T(8,128)(2,1)}) custom-call(s32[1]{0:T(128)} %bitcast.19.core_ref, f32[512,512]{1,0:T(8,128)} %get-tuple-element.224.middle, f32[16,512]{1,0:T(8,128)} %get-tuple-element.401.small, bf16[2,256,2048]{2,1,0:T(8,128)(2,1)S(1)} %copy-done, ...), custom_call_target="tpu_custom_call" | custom-call | flops 1 | bytes 1 | tf_op jit(solution)/shard_map/mlp_forward_kernel1/pallas_call | solution.py:470
  75.5 15.4 %mlp_backward_kernel1.1 = (f32[512,512]{1,0:T(8,128)}, f32[8,512]{1,0:T(8,128)}, bf16[2048,512]{1,0:T(8,128)(2,1)}, bf16[2048,512]{1,0:T(8,128)(2,1)}) custom-call(s32[1]{0:T(128)} %bitcast.19.core_ref, bf16[2,196,512]{2,1,0:T(8,128)(2,1)} %copy.62.grad, bf16[256,196]{1,0:T(8,128)(2,1)S(1)} %copy-done.11, f32[512,512]{1,0:T(8,128)} %get-tuple-element.224.middle, ...), custom_call_target="tpu_custom_call" | custom-call | flops 1 | bytes 1 | tf_op jit(solution)/shard_map/mlp_backward_kernel1/pallas_call | solution.py:470
  91.5 17.9 %attention_backward_kernel1.1 = (f32[512,512]{1,0:T(8,128)}, f32[8,512]{1,0:T(8,128)}, f32[4,64,256]{2,1,0:T(8,128)}, bf16[1024,512]{1,0:T(8,128)(2,1)}, bf16[1024,512]{1,0:T(8,128)(2,1)}) custom-call(s32[1]{0:T(128)} %bitcast.19.core_ref, f32[512,512]{1,0:T(8,128)} %get-tuple-element.231.middle_grad, f32[512,512]{1,0:T(8,128)} %get-tuple-element.223.source, ...), custom_call_target="tpu_custom_call" | custom-call | flops 1 | bytes 1 | tf_op jit(solution)/shard_map/attention_backward_kernel1/pallas_call | solution.py:470
  121.1 5.2 %merge.1 = bf16[3104,512]{1,0:T(8,128)(2,1)} custom-call(bf16[2048,512]{1,0:T(8,128)(2,1)} %get-tuple-element.229.refs_0_, bf16[2048,512]{1,0:T(8,128)(2,1)} %collective-permute-done.29.refs_1_, bf16[1024,512]{1,0:T(8,128)(2,1)} %get-tuple-element.236.refs_2_, bf16[1024,512]{1,0:T(8,128)(2,1)} %collective-permute-done.30.refs_3_, ...), custom_call_target="tpu_custom_call" | custom-call | tf_op jit(solution)/shard_map/merge/pallas_call | solution.py:974
  130.5 192.3 %conditional.1 = (bf16[512,512]{1,0:T(8,128)(2,1)}, bf16[512,512]{1,0:T(8,128)(2,1)}, bf16[512,512]{1,0:T(8,128)(2,1)}, bf16[256,512]{1,0:T(8,128)(2,1)}, bf16[2...) conditional(s32[]{:T(128)} %convert_element_type.27, () %tuple.27, ...), branch_computations={%region_0.1_spmd, %region_1.2_spmd} | conditional | flops 138554112 | bytes 106566416 | solution.py:997
  130.5 16.0 %mlp_backward_kernel0.1 = (f32[512,512]{1,0:T(8,128)}, f32[8,512]{1,0:T(8,128)}, bf16[2048,512]{1,0:T(8,128)(2,1)}, bf16[2048,512]{1,0:T(8,128)(2,1)}) custom-call(s32[1]{0:T(128)} %get-tuple-element.52.core_ref, f32[512,512]{1,0:T(8,128)} %get-tuple-element.54.grad, bf16[256,196]{1,0:T(8,128)(2,1)S(1)} %get-tuple-element.55.lay, ...), custom_call_target="tpu_custom_call" | custom-call | flops 1 | bytes 1 | tf_op jit(solution)/shard_map/cond/branch_1_fun/mlp_backward_kernel0/pallas_call | solution.py:470
  147.0 3.0 fusion.22
  152.6 4.2 %reduce_step.6 = (bf16[512,512]{1,0:T(8,128)(2,1)}, bf16[512,512]{1,0:T(8,128)(2,1)}, bf16[512,512]{1,0:T(8,128)(2,1)}, bf16[512,512]{1,0:T(8,128)(2,1)}) custom-call(s32[3]{0:T(128)S(1)} %get-tuple-element.53.bits_ref, bf16[4,256,512]{2,1,0:T(8,128)(2,1)} %bitcast.57, bf16[4,256,512]{2,1,0:T(8,128)(2,1)} %bitcast.59, bf16[4,256,512]{2,1,0:T(8,128)(2,1)} %bitcast.56, ...), custom_call_target="tpu_custom_call" | custom-call | flops 1 | bytes 1 | tf_op jit(solution)/shard_map/cond/branch_1_fun/reduce_step/pallas_call | solution.py:638
  161.4 17.4 %attention_backward_kernel0.1 = (f32[2,196,512]{2,1,0:T(8,128)}, f32[8,512]{1,0:T(8,128)}, f32[4,64,256]{2,1,0:T(8,128)}, bf16[1024,512]{1,0:T(8,128)(2,1)}, bf16[1024,512]{1,0:T(8,128)(2,1)}) custom-call(s32[1]{0:T(128)} %get-tuple-element.52.core_ref, f32[512,512]{1,0:T(8,128)} %get-tuple-element.74.middle_grad, bf16[2,196,512]{2,1,0:T(8,128)(2,1)} %copy.64.source, ...), custom_call_target="tpu_custom_call" | custom-call | flops 1 | bytes 1 | tf_op jit(solution)/shard_map/cond/branch_1_fun/attention_backward_kernel0/pallas_call | solution.py:470
  189.8 4.2 %reduce_step.7 = (bf16[256,512]{1,0:T(8,128)(2,1)}, bf16[256,512]{1,0:T(8,128)(2,1)}, bf16[256,512]{1,0:T(8,128)(2,1)}, bf16[256,512]{1,0:T(8,128)(2,1)}, bf16[2...) custom-call(s32[3]{0:T(128)S(1)} %copy-done.43, ...), custom_call_target="tpu_custom_call" | custom-call | flops 1 | bytes 1 | tf_op jit(solution)/shard_map/cond/branch_1_fun/reduce_step/pallas_call | solution.py:638
  198.0 10.8 %collective-permute-done.5.refs_1_ = bf16[256,512]{1,0:T(8,128)(2,1)S(1)} collective-permute-done((bf16[256,512]{1,0:T(8,128)(2,1)}, bf16[256,512]{1,0:T(8,128)(2,1)S(1)}, u32[]{:S(2)}, u32[]{:S(2)}) %collective-permute-start.5) | collective-permute-done | bytes 262176 | tf_op jit(solution)/shard_map/cond/branch_1_fun/ppermute | solution.py:497
  209.9 2.7 reduce_step.8
  216.2 3.4 collective-permute-done.10.refs_3_
  220.0 8.0 %collective-permute-done.9.refs_1_ = bf16[512,512]{1,0:T(8,128)(2,1)S(1)} collective-permute-done((bf16[512,512]{1,0:T(8,128)(2,1)}, bf16[512,512]{1,0:T(8,128)(2,1)S(1)}, u32[]{:S(2)}, u32[]{:S(2)}) %collective-permute-start.9) | collective-permute-done | bytes 524320 | tf_op jit(solution)/shard_map/cond/branch_1_fun/ppermute | solution.py:497
  231.4 2.6 collective-permute-start.12
  235.1 20.1 %collective-permute-done.13.refs_3_ = bf16[288,512]{1,0:T(8,128)(2,1)S(1)} collective-permute-done((bf16[288,512]{1,0:T(8,128)(2,1)}, bf16[288,512]{1,0:T(8,128)(2,1)S(1)}, u32[]{:S(2)}, u32[]{:S(2)}) %collective-permute-start.13) | collective-permute-done | bytes 294944 | tf_op jit(solution)/shard_map/cond/branch_1_fun/ppermute | solution.py:497
  255.2 7.3 %collective-permute-done.12.refs_1_ = bf16[512,512]{1,0:T(8,128)(2,1)S(1)} collective-permute-done((bf16[512,512]{1,0:T(8,128)(2,1)}, bf16[512,512]{1,0:T(8,128)(2,1)S(1)}, u32[]{:S(2)}, u32[]{:S(2)}) %collective-permute-start.12) | collective-permute-done | bytes 524320 | tf_op jit(solution)/shard_map/cond/branch_1_fun/ppermute | solution.py:497
  263.3 2.6 reduce_step.10
  268.6 31.8 %collective-permute-done.18.refs_1_ = bf16[288,512]{1,0:T(8,128)(2,1)S(1)} collective-permute-done((bf16[288,512]{1,0:T(8,128)(2,1)}, bf16[288,512]{1,0:T(8,128)(2,1)S(1)}, u32[]{:S(2)}, u32[]{:S(2)}) %collective-permute-start.18) | collective-permute-done | bytes 294944 | tf_op jit(solution)/shard_map/cond/branch_1_fun/ppermute | solution.py:497
  309.1 4.0 %collective-permute-done.19 = bf16[288,512]{1,0:T(8,128)(2,1)} collective-permute-done((bf16[288,512]{1,0:T(8,128)(2,1)}, bf16[288,512]{1,0:T(8,128)(2,1)}, u32[]{:S(2)}, u32[]{:S(2)}) %collective-permute-start.19) | collective-permute-done | bytes 294944 | tf_op jit(solution)/shard_map/cond/branch_1_fun/ppermute | solution.py:497
  322.8 7.8 %unpack.1 = (f32[2,256,1536]{2,1,0:T(8,128)}, f32[2,256,512]{2,1,0:T(8,128)}, f32[2,256,2048]{2,1,0:T(8,128)}, f32[2,1024,512]{2,1,0:T(8,128)}, f32[2,2,256]{2,1...) custom-call(s32[3]{0:T(128)} %copy-done.41, ...), custom_call_target="tpu_custom_call" | custom-call | tf_op jit(solution)/shard_map/unpack/pallas_call | solution.py:1016
  (224 shorter events, 99.0 us)
Async XLA Ops:
  7.2 315.6 %all-reduce.9.cloned.1.call-start = ((), (), s32[]{:S(2)}) async-start(), calls=%async_computation | async-start | bytes 6356992 | tf_op jit(solution)/shard_map/psum | solution.py:995
  7.3 39.4 %collective-permute-start.27 = (bf16[2,256,2048]{2,1,0:T(8,128)(2,1)}, bf16[2,256,2048]{2,1,0:T(8,128)(2,1)}, u32[]{:S(2)}, u32[]{:S(2)}) collective-permute-start(bf16[2,256,2048]{2,1,0:T(8,128)(2,1)} %up_own.5), channel_id=1, source_target_pairs={{0,1},{1,0},{2,3},{3,2},{4,5},{5,4},{6,7},{7,6},{8,9},{9,8},{10,11... | collective-permute-start | bytes 6291464 | tf_op jit(solution)/shard_map/ppermute | solution.py:488
  7.8 38.9 %collective-permute-start.28 = (bf16[2,1024,512]{2,1,0:T(8,128)(2,1)}, bf16[2,1024,512]{2,1,0:T(8,128)(2,1)}, u32[]{:S(2)}, u32[]{:S(2)}) collective-permute-start(bf16[2,1024,512]{2,1,0:T(8,128)(2,1)} %down_own.5), channel_id=1, source_target_pairs={{0,1},{1,0},{2,3},{3,2},{4,5},{5,4},{6,7},{7,6},{8,9},{9,8},{10,11... | collective-permute-start | bytes 6291464 | tf_op jit(solution)/shard_map/ppermute | solution.py:488
  11.9 18.1 %collective-permute-start.23 = (bf16[2,12,256]{2,1,0:T(8,128)(2,1)}, bf16[2,12,256]{2,1,0:T(8,128)(2,1)}, u32[]{:S(2)}, u32[]{:S(2)}) collective-permute-start(bf16[2,12,256]{2,1,0:T(8,128)(2,1)} %concatenate.27), channel_id=1, source_target_pairs={{0,1},{1,0},{2,3},{3,2},{4,5},{5,4},{6,7},{7,6},{8,9},{9,8},{10,11... | collective-permute-start | bytes 36872 | tf_op jit(solution)/shard_map/ppermute | solution.py:488
  12.4 21.1 %collective-permute-start.25 = (bf16[2,256,1536]{2,1,0:T(8,128)(2,1)}, bf16[2,256,1536]{2,1,0:T(8,128)(2,1)S(1)}, u32[]{:S(2)}, u32[]{:S(2)}) collective-permute-start(bf16[2,256,1536]{2,1,0:T(8,128)(2,1)} %qkv_own.5), channel_id=1, source_target_pairs={{0,1},{1,0},{2,3},{3,2},{4,5},{5,4},{6,7},{7,6},{8,9},{9,8},{10,11... | collective-permute-start | bytes 4718600 | tf_op jit(solution)/shard_map/ppermute | solution.py:488
  22.0 11.5 %collective-permute-start.26 = (bf16[2,256,512]{2,1,0:T(8,128)(2,1)S(1)}, bf16[2,256,512]{2,1,0:T(8,128)(2,1)S(1)}, u32[]{:S(2)}, u32[]{:S(2)}) collective-permute-start(bf16[2,256,512]{2,1,0:T(8,128)(2,1)S(1)} %copy-done.8), channel_id=1, source_target_pairs={{0,1},{1,0},{2,3},{3,2},{4,5},{5,4},{6,7},{7,6},{8,9},{9,8},{10,11... | collective-permute-start | bytes 1572872 | tf_op jit(solution)/shard_map/ppermute | solution.py:488
  91.0 29.5 %collective-permute-start.29 = (bf16[2048,512]{1,0:T(8,128)(2,1)}, bf16[2048,512]{1,0:T(8,128)(2,1)}, u32[]{:S(2)}, u32[]{:S(2)}) collective-permute-start(bf16[2048,512]{1,0:T(8,128)(2,1)} %get-tuple-element.230), channel_id=1, source_target_pairs={{0,1},{1,0},{2,3},{3,2},{4,5},{5,4},{6,7},{7,6},{8,9},{9,8},{10,11... | collective-permute-start | bytes 6291464 | tf_op jit(solution)/shard_map/ppermute | solution.py:488
  109.3 11.1 %collective-permute-start.30 = (bf16[1024,512]{1,0:T(8,128)(2,1)}, bf16[1024,512]{1,0:T(8,128)(2,1)}, u32[]{:S(2)}, u32[]{:S(2)}) collective-permute-start(bf16[1024,512]{1,0:T(8,128)(2,1)} %get-tuple-element.237), channel_id=1, source_target_pairs={{0,1},{1,0},{2,3},{3,2},{4,5},{5,4},{6,7},{7,6},{8,9},{9,8},{10,11... | collective-permute-start | bytes 3145736 | tf_op jit(solution)/shard_map/ppermute | solution.py:488
  156.8 22.0 %collective-permute-start.1 = (bf16[512,512]{1,0:T(8,128)(2,1)}, bf16[512,512]{1,0:T(8,128)(2,1)}, u32[]{:S(2)}, u32[]{:S(2)}) collective-permute-start(bf16[512,512]{1,0:T(8,128)(2,1)} %get-tuple-element.72), channel_id=1, source_target_pairs={{0,2},{2,0},{4,6},{6,4},{8,10},{10,8},{12,14},{14,12},{16,18},{18,... | collective-permute-start | bytes 1572872 | tf_op jit(solution)/shard_map/cond/branch_1_fun/ppermute | solution.py:497
  159.0 19.8 %collective-permute-start.2 = (bf16[512,512]{1,0:T(8,128)(2,1)}, bf16[512,512]{1,0:T(8,128)(2,1)}, u32[]{:S(2)}, u32[]{:S(2)}) collective-permute-start(bf16[512,512]{1,0:T(8,128)(2,1)} %get-tuple-element.94), channel_id=1, source_target_pairs={{0,4},{2,6},{4,0},{6,2},{8,12},{10,14},{12,8},{14,10},{16,20},{18,... | collective-permute-start | bytes 1572872 | tf_op jit(solution)/shard_map/cond/branch_1_fun/ppermute | solution.py:497
  194.0 14.9 %collective-permute-start.7 = (bf16[288,512]{1,0:T(8,128)(2,1)}, bf16[288,512]{1,0:T(8,128)(2,1)S(1)}, u32[]{:S(2)}, u32[]{:S(2)}) collective-permute-start(bf16[288,512]{1,0:T(8,128)(2,1)} %get-tuple-element.120), channel_id=1, source_target_pairs={{0,2},{2,0},{4,6},{6,4},{8,10},{10,8},{12,14},{14,12},{16,18},{18,... | collective-permute-start | bytes 884744 | tf_op jit(solution)/shard_map/cond/branch_1_fun/ppermute | solution.py:497
  194.4 14.5 %collective-permute-start.8 = (bf16[288,512]{1,0:T(8,128)(2,1)}, bf16[288,512]{1,0:T(8,128)(2,1)S(1)}, u32[]{:S(2)}, u32[]{:S(2)}) collective-permute-start(bf16[288,512]{1,0:T(8,128)(2,1)} %get-tuple-element.122), channel_id=1, source_target_pairs={{0,4},{2,6},{4,0},{6,2},{8,12},{10,14},{12,8},{14,10},{16,20},{18,... | collective-permute-start | bytes 884744 | tf_op jit(solution)/shard_map/cond/branch_1_fun/ppermute | solution.py:497
  194.4 14.4 %collective-permute-start.5 = (bf16[256,512]{1,0:T(8,128)(2,1)}, bf16[256,512]{1,0:T(8,128)(2,1)S(1)}, u32[]{:S(2)}, u32[]{:S(2)}) collective-permute-start(bf16[256,512]{1,0:T(8,128)(2,1)} %get-tuple-element.115), channel_id=1, source_target_pairs={{0,4},{2,6},{4,0},{6,2},{8,12},{10,14},{12,8},{14,10},{16,20},{18,... | collective-permute-start | bytes 786440 | tf_op jit(solution)/shard_map/cond/branch_1_fun/ppermute | solution.py:497
  196.4 12.5 %collective-permute-start.6 = (bf16[256,512]{1,0:T(8,128)(2,1)}, bf16[256,512]{1,0:T(8,128)(2,1)S(1)}, u32[]{:S(2)}, u32[]{:S(2)}) collective-permute-start(bf16[256,512]{1,0:T(8,128)(2,1)} %get-tuple-element.118), channel_id=1, source_target_pairs={{0,2},{2,0},{4,6},{6,4},{8,10},{10,8},{12,14},{14,12},{16,18},{18,... | collective-permute-start | bytes 786440 | tf_op jit(solution)/shard_map/cond/branch_1_fun/ppermute | solution.py:497
  212.6 15.5 %collective-permute-start.9 = (bf16[512,512]{1,0:T(8,128)(2,1)}, bf16[512,512]{1,0:T(8,128)(2,1)S(1)}, u32[]{:S(2)}, u32[]{:S(2)}) collective-permute-start(bf16[512,512]{1,0:T(8,128)(2,1)} %get-tuple-element.136.refs_0_), channel_id=1, source_target_pairs={{0,8},{2,10},{4,12},{6,14},{8,0},{10,2},{12,4},{14,6},{16,24},{18,... | collective-permute-start | bytes 1572872 | tf_op jit(solution)/shard_map/cond/branch_1_fun/ppermute | solution.py:497
  231.4 31.1 %collective-permute-start.12 = (bf16[512,512]{1,0:T(8,128)(2,1)}, bf16[512,512]{1,0:T(8,128)(2,1)S(1)}, u32[]{:S(2)}, u32[]{:S(2)}) collective-permute-start(bf16[512,512]{1,0:T(8,128)(2,1)} %get-tuple-element.144.refs_0_), channel_id=1, source_target_pairs={{0,16},{2,18},{4,20},{6,22},{8,24},{10,26},{12,28},{14,30},{16,0},... | collective-permute-start | bytes 1572872 | tf_op jit(solution)/shard_map/cond/branch_1_fun/ppermute | solution.py:497
  234.0 21.2 %collective-permute-start.13 = (bf16[288,512]{1,0:T(8,128)(2,1)}, bf16[288,512]{1,0:T(8,128)(2,1)S(1)}, u32[]{:S(2)}, u32[]{:S(2)}) collective-permute-start(bf16[288,512]{1,0:T(8,128)(2,1)} %get-tuple-element.146.refs_2_), channel_id=1, source_target_pairs={{0,8},{2,10},{4,12},{6,14},{8,0},{10,2},{12,4},{14,6},{16,24},{18,... | collective-permute-start | bytes 884744 | tf_op jit(solution)/shard_map/cond/branch_1_fun/ppermute | solution.py:497
  265.9 39.4 %collective-permute-start.14 = (bf16[512,512]{1,0:T(8,128)(2,1)}, bf16[512,512]{1,0:T(8,128)(2,1)}, u32[]{:S(2)}, u32[]{:S(2)}) collective-permute-start(bf16[512,512]{1,0:T(8,128)(2,1)} %get-tuple-element.420), channel_id=1, source_target_pairs={{0,2},{2,0},{4,6},{6,4},{8,10},{10,8},{12,14},{14,12},{16,18},{18,... | collective-permute-start | bytes 1572872 | tf_op jit(solution)/shard_map/cond/branch_1_fun/ppermute | solution.py:497
  267.3 38.0 %collective-permute-start.15 = (bf16[512,512]{1,0:T(8,128)(2,1)}, bf16[512,512]{1,0:T(8,128)(2,1)}, u32[]{:S(2)}, u32[]{:S(2)}) collective-permute-start(bf16[512,512]{1,0:T(8,128)(2,1)} %get-tuple-element.420), channel_id=1, source_target_pairs={{0,4},{2,6},{4,0},{6,2},{8,12},{10,14},{12,8},{14,10},{16,20},{18,... | collective-permute-start | bytes 1572872 | tf_op jit(solution)/shard_map/cond/branch_1_fun/ppermute | solution.py:497
  268.6 31.8 %collective-permute-start.18 = (bf16[288,512]{1,0:T(8,128)(2,1)}, bf16[288,512]{1,0:T(8,128)(2,1)S(1)}, u32[]{:S(2)}, u32[]{:S(2)}) collective-permute-start(bf16[288,512]{1,0:T(8,128)(2,1)} %get-tuple-element.153.refs_0_), channel_id=1, source_target_pairs={{0,16},{2,18},{4,20},{6,22},{8,24},{10,26},{12,28},{14,30},{16,0},... | collective-permute-start | bytes 884744 | tf_op jit(solution)/shard_map/cond/branch_1_fun/ppermute | solution.py:497
  303.0 10.2 %collective-permute-start.19 = (bf16[288,512]{1,0:T(8,128)(2,1)}, bf16[288,512]{1,0:T(8,128)(2,1)}, u32[]{:S(2)}, u32[]{:S(2)}) collective-permute-start(bf16[288,512]{1,0:T(8,128)(2,1)} %reduce_step.11), channel_id=1, source_target_pairs={{0,2},{2,0},{4,6},{6,4},{8,10},{10,8},{12,14},{14,12},{16,18},{18,... | collective-permute-start | bytes 884744 | tf_op jit(solution)/shard_map/cond/branch_1_fun/ppermute | solution.py:497
  304.1 10.3 %collective-permute-start.20 = (bf16[288,512]{1,0:T(8,128)(2,1)}, bf16[288,512]{1,0:T(8,128)(2,1)}, u32[]{:S(2)}, u32[]{:S(2)}) collective-permute-start(bf16[288,512]{1,0:T(8,128)(2,1)} %reduce_step.11), channel_id=1, source_target_pairs={{0,4},{2,6},{4,0},{6,2},{8,12},{10,14},{12,8},{14,10},{16,20},{18,... | collective-permute-start | bytes 884744 | tf_op jit(solution)/shard_map/cond/branch_1_fun/ppermute | solution.py:497
  306.3 16.5 %collective-permute-start.16 = (bf16[256,512]{1,0:T(8,128)(2,1)S(1)}, bf16[256,512]{1,0:T(8,128)(2,1)}, u32[]{:S(2)}, u32[]{:S(2)}) collective-permute-start(bf16[256,512]{1,0:T(8,128)(2,1)S(1)} %slice.52), channel_id=1, source_target_pairs={{0,4},{2,6},{4,0},{6,2},{8,12},{10,14},{12,8},{14,10},{16,20},{18,... | collective-permute-start | bytes 786440 | tf_op jit(solution)/shard_map/cond/branch_1_fun/ppermute | solution.py:497
  308.2 14.6 %collective-permute-start.17 = (bf16[256,512]{1,0:T(8,128)(2,1)S(1)}, bf16[256,512]{1,0:T(8,128)(2,1)}, u32[]{:S(2)}, u32[]{:S(2)}) collective-permute-start(bf16[256,512]{1,0:T(8,128)(2,1)S(1)} %slice.53), channel_id=1, source_target_pairs={{0,2},{2,0},{4,6},{6,4},{8,10},{10,8},{12,14},{14,12},{16,18},{18,... | collective-permute-start | bytes 786440 | tf_op jit(solution)/shard_map/cond/branch_1_fun/ppermute | solution.py:497
  (56 other events, 502.7 us)
Sparse Core Ops, SparseCore 0:
  126.4 177.8 all-reduce.8
where the time goes:
time: 340 us; the launch traced here: 339 us
  Pallas kernels  138 us (41%)
  waiting for transfers between devices  91.8 us (27%)
  local copies, waits for them, and re-layouts  54.6 us (16%)
  starting transfers between devices  28.2 us (8%)
  between operations  14.4 us (4%)
  other arithmetic  5.8 us (2%)
  matrix products  5.26 us (2%)
    pallas_call x8, Pallas kernels, call(): pl.pallas_call(functools.partial(kernel, layer, rows), in_specs=[pl.Block...  107 us
    ppermute x20, waiting for transfers between devices, dp_swap(): lax.ppermute(value, 'dp', [(at, at ^ 1 << bit) for at in range(count)])  89.9 us
    ppermute x20, starting transfers between devices, dp_swap(): lax.ppermute(value, 'dp', [(at, at ^ 1 << bit) for at in range(count)])  24.3 us
    pallas_call x6, Pallas kernels, advance(): pl.pallas_call(functools.partial(step_kernel, plan), in_specs=[pl.BlockSp...  18.1 us
    reshape x6, local copies, waits for them, and re-layouts, small_rows(): pairs.reshape(QUADS, ROWS, 4, ROWS).transpose(0, 2, 1, 3).reshape(HEADS, -1)  9.06 us
    pallas_call x1, Pallas kernels, body(): pl.pallas_call(unpack_kernel, in_specs=[pl.BlockSpec(memory_space=pltpu.S...  7.81 us
  transfers between devices with their start and end apart: 33, of which 13 were waited for; matrix products, arithmetic and copies ran while one was open for 17% of the time, Pallas kernels for 24%

commit v1 on v0

--- a/solution.py
+++ b/solution.py
@@ -222,7 +222,7 @@
             queries = stack_heads(qkv[part, lanes], masks)
             keys = qkv[part, D + quad * 128 : D + (quad + 1) * 128]
             values = qkv[part, 2 * D + quad * 128 : 2 * D + (quad + 1) * 128]
-            scores = scale * dot_nt(keys, queries) + bias[quad]
+            scores = scale * dot_nt(keys, queries) + bias[layer, quad]
             if layer:
                 scores = scores + mask[at % 4]
             expo = jnp.exp(scores - jnp.max(scores, 0, keepdims=True))
@@ -474,7 +474,7 @@
         out_specs=[pl.BlockSpec(memory_space=spaces[kind]) for kind in out_kinds],
         out_shape=outs,
         scratch_shapes=scratch,
-        compiler_params=pltpu.CompilerParams(vmem_limit_bytes=56 * 1024 * 1024),
+        compiler_params=pltpu.CompilerParams(vmem_limit_bytes=30 * 1024 * 1024),
         cost_estimate=pl.CostEstimate(flops=1, bytes_accessed=1, transcendentals=0),
         name=kernel.__name__ + str(layer),
     )(core, *inputs)
@@ -641,7 +641,7 @@
         + [pl.BlockSpec(memory_space=pltpu.VMEM)] * len(inputs),
         out_specs=[pl.BlockSpec(memory_space=pltpu.VMEM)] * len(outs),
         out_shape=outs,
-        compiler_params=pltpu.CompilerParams(vmem_limit_bytes=56 * 1024 * 1024),
+        compiler_params=pltpu.CompilerParams(vmem_limit_bytes=30 * 1024 * 1024),
         cost_estimate=pl.CostEstimate(flops=1, bytes_accessed=1, transcendentals=0),
         name="reduce_step",
     )(bits, *inputs)
@@ -692,7 +692,7 @@
             4 * D + at * half : 4 * D + (at + 1) * half, :
         ].astype(f32)
     proj_out[1] = upper[4 * D + 3 * half : 6 * D, :].astype(f32)
-    tiny[1] = upper[6 * D :, :].astype(f32)
+    tiny[1, :16, :] = upper[6 * D :, :].astype(f32)
     quarters(mlp_in, x, y, mlp)
     quarters(attn_in, x, y, attn)
     for at in range(4):
@@ -708,6 +708,7 @@
             proj_out[0, rows, :] = value
     for at in range(2):
         tiny[0, at * 16 : (at + 1) * 16, :] = attn[at, q : q + 16, :].astype(f32)
+    tiny[1, 16:, :] = attn[2, q : q + 16, :].astype(f32)
     first = core == 0
 
     def own(row):
@@ -821,7 +822,7 @@
                 to_moved,
                 from_moved,
                 small,
-                bias_all[layer],
+                bias_all,
                 mask,
                 qkv_weight,
                 qkv_other,
@@ -863,13 +864,14 @@
     bits = jnp.stack([at_dp & 1, (at_dp >> 1) & 1, lax.axis_index("fsdp")]).astype(jnp.int32)
     onehot_f = onehot.astype(f32)
 
-    def small_rows(attn_sums, mlp_sums, pairs):
-        flat = pairs.reshape(QUADS, ROWS, 4, ROWS).transpose(0, 2, 1, 3).reshape(HEADS, -1)
-        heads = jnp.einsum("hp,rp->hr", flat, onehot_f, precision=lax.Precision.HIGHEST)
-        heads = jnp.pad(heads, ((0, 0), (0, D - LIVE)))
-        return jnp.concatenate([attn_sums, mlp_sums, heads], axis=0).astype(bf16)
-
-    def backward(layer, grad, kept):
+    def table_rows(pairs):
+        flat = (
+            pairs.reshape(2, QUADS, ROWS, 4, ROWS).transpose(0, 1, 3, 2, 4).reshape(2 * HEADS, -1)
+        )
+        heads = jnp.einsum("hp,rp->hr", flat, onehot_f, precision=lax.Precision.HIGH)
+        return jnp.pad(heads, ((0, 0), (0, D - LIVE)))
+
+    def backward(layer, grad, kept, pairs_upper=None):
         source, middle, normed, qkv, probs, mixed, normed_two, hidden, slope, small = kept
         middle_grad, mlp_sums, mlp_keep, mlp_send = call(
             mlp_backward_kernel,
@@ -968,17 +970,20 @@
                 lax.optimization_barrier(held)
             )
         attn_got = swap_cores(attn_send)
-        tiny = small_rows(attn_sums, mlp_sums, pairs)
+        tiny = [attn_sums, mlp_sums]
+        if layer == 0:
+            tiny.append(table_rows(jnp.stack([pairs, pairs_upper])))
+        tiny = jnp.concatenate(tiny, axis=0).astype(bf16)
         tiny_got = swap_cores(tiny)
         if layer == 1:
             upper = pl.pallas_call(
                 merge_kernel,
-                out_shape=shape((6 * D + 32, D), bf16),
-                compiler_params=pltpu.CompilerParams(vmem_limit_bytes=56 * 1024 * 1024),
+                out_shape=shape((6 * D + 16, D), bf16),
+                compiler_params=pltpu.CompilerParams(vmem_limit_bytes=30 * 1024 * 1024),
                 name="merge",
             )(mlp_keep, mlp_got, attn_keep, attn_got, tiny, tiny_got)
-            return lax.optimization_barrier((upper, grad))
-        pad = ((0, 96), (0, 0))
+            return lax.optimization_barrier((upper, grad, pairs))
+        pad = ((0, 80), (0, 0))
         attn_group = Group(
             D,
             [(attn_keep[:D], attn_got[:D]), (attn_keep[D:], attn_got[D:])],
@@ -991,9 +996,9 @@
             mark = advance([group for group in groups if not group.done], bits, mark)
         return [grad] + mlp_group.state + attn_group.state
 
-    upper, grad = backward(1, cotangent, saved[1])
+    upper, grad, pairs_upper = backward(1, cotangent, saved[1])
     upper = lax.psum(upper, "dp")
-    taken = (grad, saved[0])
+    taken = (grad, saved[0], pairs_upper)
     grad, *arrived = lax.cond(
         lax.optimization_barrier(jnp.bool_(True)),
         lambda taken: backward(0, *taken),
@@ -1039,7 +1044,7 @@
             vmem((8, D // 4 + 16, D), bf16),
             vmem((2, 32, D), f32),
         ],
-        compiler_params=pltpu.CompilerParams(vmem_limit_bytes=56 * 1024 * 1024),
+        compiler_params=pltpu.CompilerParams(vmem_limit_bytes=30 * 1024 * 1024),
         name="unpack",
     )(bits, *pieces)
     table_g = heads[:, :, :RELS].transpose(0, 2, 1)

time: 340 us -> 293 us (0.86)
  Pallas kernels: 138 us -> 103 us
  local copies, waits for them, and re-layouts: 54.6 us -> 38 us
  waiting for transfers between devices: 91.8 us -> 98.2 us
    pallas_call x8, Pallas kernels: 107 us -> 87.5 us  [call(): pl.pallas_call(functools.partial(kernel, layer, rows), in_specs=[pl.Block...]
    pallas_call x6, Pallas kernels: 18.1 us -> 6.4 us  [advance(): pl.pallas_call(functools.partial(step_kernel, plan), in_specs=[pl.BlockSp...]
    another operation x1 -> x5, local copies, waits for them, and re-layouts: 0.82 us -> 7.01 us  [the longest x4 6.96 us: backward(): tiny.append(table_rows(jnp.stack([pairs, pairs_upper])))]
    ppermute x12, waiting for transfers between devices: 1.83 us -> 6.78 us  [swap_cores(): return lax.ppermute(value, 'fsdp', [(0, 1), (1, 0)])]
    reshape x6 -> x2, local copies, waits for them, and re-layouts: 9.06 us -> 4.22 us  [the longest x1 2.38 us: table_rows(): pairs.reshape(2, QUADS, ROWS, 4, ROWS).transpose(0, 1, 3, 2, 4)]
  transfers between devices with their start and end apart: 33 -> 33, of which waited for: 13 -> 12; matrix products, arithmetic and copies ran while one was open for 17% -> 14% of each run, Pallas kernels for 24% -> 21%
where the time goes in v1:
time: 293 us; the launch traced here: 292 us
  Pallas kernels  103 us (35%)
  waiting for transfers between devices  98.2 us (34%)
  local copies, waits for them, and re-layouts  38 us (13%)
  starting transfers between devices  29.2 us (10%)
  between operations  14.5 us (5%)
  other arithmetic  5.12 us (2%)
  matrix products  4.04 us (1%)
    ppermute x20, waiting for transfers between devices, dp_swap(): lax.ppermute(value, 'dp', [(at, at ^ 1 << bit) for at in range(count)])  91.4 us
    pallas_call x8, Pallas kernels, call(): pl.pallas_call(functools.partial(kernel, layer, rows), in_specs=[pl.Block...  87.5 us
    ppermute x20, starting transfers between devices, dp_swap(): lax.ppermute(value, 'dp', [(at, at ^ 1 << bit) for at in range(count)])  25.5 us
    another operation x4, local copies, waits for them, and re-layouts, backward(): tiny.append(table_rows(jnp.stack([pairs, pairs_upper])))  6.96 us
    ppermute x12, waiting for transfers between devices, swap_cores(): return lax.ppermute(value, 'fsdp', [(0, 1), (1, 0)])  6.78 us
    pallas_call x1, Pallas kernels, body(): pl.pallas_call(unpack_kernel, in_specs=[pl.BlockSpec(memory_space=pltpu.S...  6.73 us
    pallas_call x6, Pallas kernels, advance(): pl.pallas_call(functools.partial(step_kernel, plan), in_specs=[pl.BlockSp...  6.4 us
  transfers between devices with their start and end apart: 33, of which 12 were waited for; matrix products, arithmetic and copies ran while one was open for 14% of the time, Pallas kernels for 21%

profile of v1, /device:TPU:0, one launch (start us, length us, event | category | flops | bytes accessed | tf_op | source)
XLA Modules:
  0.0 292.3 jit_solution(10311990358279140556)
XLA Ops:
  19.6 3.0 %copy.72 = f32[2,4,4,64,64]{4,2,3,1,0:T(4,128)} copy(f32[2,4,4,64,64]{4,3,2,1,0:T(8,128)} %reshape.130) | data formatting | bytes 1048576 | tf_op jit(solution)/shard_map/reshape | solution.py:790
  25.3 11.5 %attention_forward_kernel0.1 = (f32[512,512]{1,0:T(8,128)S(1)}, bf16[512,512]{1,0:T(8,128)(2,1)}, bf16[512,1536]{1,0:T(8,128)(2,1)}, f32[8,4,64,256]{3,2,1,0:T(8,128)}, bf16[512,512]{1,0:T(8,128)(2,1)}) custom-call(s32[1]{0:T(128)} %bitcast.19.core_ref, bf16[2,196,512]{2,1,0:T(8,128)(2,1)S(1)} %copy.60.source, bf16[256,196]{1,0:T(8,128)(2,1)S(1)} %copy-done.11, ...), custom_call_target="tpu_custom_call" | custom-call | flops 1 | bytes 1 | tf_op jit(solution)/shard_map/attention_forward_kernel0/pallas_call | solution.py:470
  36.9 7.3 %mlp_forward_kernel0.1 = (f32[512,512]{1,0:T(8,128)S(1)}, bf16[512,512]{1,0:T(8,128)(2,1)}, bf16[512,2048]{1,0:T(8,128)(2,1)}, bf16[512,2048]{1,0:T(8,128)(2,1)}) custom-call(s32[1]{0:T(128)} %bitcast.19.core_ref, f32[512,512]{1,0:T(8,128)S(1)} %get-tuple-element.226.middle, f32[16,512]{1,0:T(8,128)S(1)} %get-tuple-element.408.small, ...), custom_call_target="tpu_custom_call" | custom-call | flops 1 | bytes 1 | tf_op jit(solution)/shard_map/mlp_forward_kernel0/pallas_call | solution.py:470
  44.2 8.8 %attention_forward_kernel1.1 = (f32[512,512]{1,0:T(8,128)S(1)}, bf16[512,512]{1,0:T(8,128)(2,1)S(1)}, bf16[512,1536]{1,0:T(8,128)(2,1)S(1)}, f32[8,4,64,256]{3,2,1,0:T(8,128)S(1)}, bf16[512,512]{1,0:T(8,128)(2,1)S(1)}) custom-call(s32[1]{0:T(128)} %bitcast.19.core_ref, f32[512,512]{1,0:T(8,128)S(1)} %get-tuple-element.227.source, ...), custom_call_target="tpu_custom_call" | custom-call | flops 1 | bytes 1 | tf_op jit(solution)/shard_map/attention_forward_kernel1/pallas_call | solution.py:470
  53.1 6.1 %mlp_forward_kernel1.1 = (f32[512,512]{1,0:T(8,128)S(1)}, bf16[512,512]{1,0:T(8,128)(2,1)S(1)}, bf16[512,2048]{1,0:T(8,128)(2,1)S(1)}, bf16[512,2048]{1,0:T(8,128)(2,1)S(1)}) custom-call(s32[1]{0:T(128)} %bitcast.19.core_ref, f32[512,512]{1,0:T(8,128)S(1)} %get-tuple-element.228.middle, f32[16,512]{1,0:T(8,128)S(1)} %get-tuple-element.407.small, ...), custom_call_target="tpu_custom_call" | custom-call | flops 1 | bytes 1 | tf_op jit(solution)/shard_map/mlp_forward_kernel1/pallas_call | solution.py:470
  59.2 10.2 %mlp_backward_kernel1.1 = (f32[512,512]{1,0:T(8,128)S(1)}, f32[8,512]{1,0:T(8,128)S(1)}, bf16[2048,512]{1,0:T(8,128)(2,1)S(1)}, bf16[2048,512]{1,0:T(8,128)(2,1)S(1)}) custom-call(s32[1]{0:T(128)} %bitcast.19.core_ref, bf16[2,196,512]{2,1,0:T(8,128)(2,1)S(1)} %copy.63.grad, bf16[256,196]{1,0:T(8,128)(2,1)S(1)} %copy-done.12, ...), custom_call_target="tpu_custom_call" | custom-call | flops 1 | bytes 1 | tf_op jit(solution)/shard_map/mlp_backward_kernel1/pallas_call | solution.py:470
  69.9 15.1 %attention_backward_kernel1.1 = (f32[512,512]{1,0:T(8,128)}, f32[8,512]{1,0:T(8,128)S(1)}, f32[4,64,256]{2,1,0:T(8,128)}, bf16[1024,512]{1,0:T(8,128)(2,1)S(1)}, bf16[1024,512]{1,0:T(8,128)(2,1)S(1)}) custom-call(s32[1]{0:T(128)} %bitcast.19.core_ref, f32[512,512]{1,0:T(8,128)S(1)} %get-tuple-element.235.middle_grad, ...), custom_call_target="tpu_custom_call" | custom-call | flops 1 | bytes 1 | tf_op jit(solution)/shard_map/attention_backward_kernel1/pallas_call | solution.py:470
  87.8 2.4 merge.1
  95.2 181.0 %conditional.1 = (bf16[512,512]{1,0:T(8,128)(2,1)}, bf16[512,512]{1,0:T(8,128)(2,1)}, bf16[512,512]{1,0:T(8,128)(2,1)}, bf16[256,512]{1,0:T(8,128)(2,1)}, bf16[2...) conditional(s32[]{:T(128)} %convert_element_type.26, () %tuple.27, ...), branch_computations={%region_0.1_spmd, %region_1.2_spmd} | conditional | flops 138753536 | bytes 101629240 | solution.py:1002
  95.2 13.3 %mlp_backward_kernel0.1 = (f32[512,512]{1,0:T(8,128)S(1)}, f32[8,512]{1,0:T(8,128)S(1)}, bf16[2048,512]{1,0:T(8,128)(2,1)S(1)}, bf16[2048,512]{1,0:T(8,128)(2,1)S(1)}) custom-call(s32[1]{0:T(128)} %get-tuple-element.54.core_ref, f32[512,512]{1,0:T(8,128)S(1)} %get-tuple-element.56.grad, bf16[256,196]{1,0:T(8,128)(2,1)S(1)} %get-tuple-element.57.lay, ...), custom_call_target="tpu_custom_call" | custom-call | flops 1 | bytes 1 | tf_op jit(solution)/shard_map/cond/branch_1_fun/mlp_backward_kernel0/pallas_call | solution.py:470
  108.9 3.9 %collective-permute-done = bf16[2048,512]{1,0:T(8,128)(2,1)S(1)} collective-permute-done((bf16[2048,512]{1,0:T(8,128)(2,1)S(1)}, bf16[2048,512]{1,0:T(8,128)(2,1)S(1)}, u32[]{:S(2)}, u32[]{:S(2)}) %collective-permute-start) | collective-permute-done | bytes 2097184 | tf_op jit(solution)/shard_map/cond/branch_1_fun/ppermute | solution.py:488
  114.0 3.4 %collective-permute-start.1 = (bf16[512,512]{1,0:T(8,128)(2,1)S(1)}, bf16[512,512]{1,0:T(8,128)(2,1)S(1)}, u32[]{:S(2)}, u32[]{:S(2)}) collective-permute-start(bf16[512,512]{1,0:T(8,128)(2,1)S(1)} %get-tuple-element.74), channel_id=1, source_target_pairs={{0,2},{2,0},{4,6},{6,4},{8,10},{10,8},{12,14},{14,12},{16,18},{18,... | collective-permute-start | bytes 1572872 | tf_op jit(solution)/shard_map/cond/branch_1_fun/ppermute | solution.py:497
  119.0 15.2 %attention_backward_kernel0.1 = (f32[2,196,512]{2,1,0:T(8,128)S(1)}, f32[8,512]{1,0:T(8,128)S(1)}, f32[4,64,256]{2,1,0:T(8,128)S(1)}, bf16[1024,512]{1,0:T(8,128)(2,1)S(1)}, bf16[1024,512]{1,0:T(8,128)(2,1)}) custom-call(s32[1]{0:T(128)} %get-tuple-element.54.core_ref, f32[512,512]{1,0:T(8,128)S(1)} %get-tuple-element.76.middle_grad, ...), custom_call_target="tpu_custom_call" | custom-call | flops 1 | bytes 1 | tf_op jit(solution)/shard_map/cond/branch_1_fun/attention_backward_kernel0/pallas_call | solution.py:470
  147.2 3.4 %convolution_convert_fusion = bf16[32,176]{1,0:T(8,128)(2,1)S(1)} fusion(f32[32,4096]{1,0:T(8,128)} %reshape.109, f32[176,4096]{1,0:T(8,128)} %get-tuple-element.107), kind=kOutput, calls=%fused_computation | convolution fusion | flops 138417664 | bytes 3419136 | tf_op jit(solution)/shard_map/cond/branch_1_fun/hp,rp->hr/dot_general | solution.py:871
  158.7 11.0 %collective-permute-done.5.refs_1_ = bf16[256,512]{1,0:T(8,128)(2,1)S(1)} collective-permute-done((bf16[256,512]{1,0:T(8,128)(2,1)S(1)}, bf16[256,512]{1,0:T(8,128)(2,1)S(1)}, u32[]{:S(2)}, u32[]{:S(2)}) %collective-permute-start.5) | collective-permute-done | bytes 262176 | tf_op jit(solution)/shard_map/cond/branch_1_fun/ppermute | solution.py:497
  174.1 5.0 %collective-permute-done.10.refs_3_ = bf16[144,512]{1,0:T(8,128)(2,1)S(1)} collective-permute-done((bf16[144,512]{1,0:T(8,128)(2,1)S(1)}, bf16[144,512]{1,0:T(8,128)(2,1)S(1)}, u32[]{:S(2)}, u32[]{:S(2)}) %collective-permute-start.10) | collective-permute-done | bytes 147488 | tf_op jit(solution)/shard_map/cond/branch_1_fun/ppermute | solution.py:497
  179.1 7.8 %collective-permute-done.9.refs_1_ = bf16[512,512]{1,0:T(8,128)(2,1)S(1)} collective-permute-done((bf16[512,512]{1,0:T(8,128)(2,1)S(1)}, bf16[512,512]{1,0:T(8,128)(2,1)S(1)}, u32[]{:S(2)}, u32[]{:S(2)}) %collective-permute-start.9) | collective-permute-done | bytes 524320 | tf_op jit(solution)/shard_map/cond/branch_1_fun/ppermute | solution.py:497
  187.7 2.9 collective-permute-start.12
  191.8 21.6 %collective-permute-done.13.refs_3_ = bf16[288,512]{1,0:T(8,128)(2,1)S(1)} collective-permute-done((bf16[288,512]{1,0:T(8,128)(2,1)S(1)}, bf16[288,512]{1,0:T(8,128)(2,1)S(1)}, u32[]{:S(2)}, u32[]{:S(2)}) %collective-permute-start.13) | collective-permute-done | bytes 294944 | tf_op jit(solution)/shard_map/cond/branch_1_fun/ppermute | solution.py:497
  213.5 5.6 %collective-permute-done.12.refs_1_ = bf16[512,512]{1,0:T(8,128)(2,1)S(1)} collective-permute-done((bf16[512,512]{1,0:T(8,128)(2,1)S(1)}, bf16[512,512]{1,0:T(8,128)(2,1)S(1)}, u32[]{:S(2)}, u32[]{:S(2)}) %collective-permute-start.12) | collective-permute-done | bytes 524320 | tf_op jit(solution)/shard_map/cond/branch_1_fun/ppermute | solution.py:497
  222.1 33.6 %collective-permute-done.18.refs_1_ = bf16[288,512]{1,0:T(8,128)(2,1)S(1)} collective-permute-done((bf16[288,512]{1,0:T(8,128)(2,1)S(1)}, bf16[288,512]{1,0:T(8,128)(2,1)S(1)}, u32[]{:S(2)}, u32[]{:S(2)}) %collective-permute-start.18) | collective-permute-done | bytes 294944 | tf_op jit(solution)/shard_map/cond/branch_1_fun/ppermute | solution.py:497
  263.1 3.8 %collective-permute-done.19 = bf16[288,512]{1,0:T(8,128)(2,1)} collective-permute-done((bf16[288,512]{1,0:T(8,128)(2,1)}, bf16[288,512]{1,0:T(8,128)(2,1)}, u32[]{:S(2)}, u32[]{:S(2)}) %collective-permute-start.19) | collective-permute-done | bytes 294944 | tf_op jit(solution)/shard_map/cond/branch_1_fun/ppermute | solution.py:497
  273.7 2.5 collective-permute-done.22
  278.1 6.7 %unpack.1 = (f32[2,256,1536]{2,1,0:T(8,128)}, f32[2,256,512]{2,1,0:T(8,128)}, f32[2,256,2048]{2,1,0:T(8,128)}, f32[2,1024,512]{2,1,0:T(8,128)}, f32[2,2,256]{2,1...) custom-call(s32[3]{0:T(128)S(1)} %pad_add_fusion.bits_ref, ...), custom_call_target="tpu_custom_call" | custom-call | tf_op jit(solution)/shard_map/unpack/pallas_call | solution.py:1021
  (199 shorter events, 73.4 us)
Async XLA Ops:
  7.2 269.0 %all-reduce.8.cloned.1.call-start = ((), (), s32[]{:S(2)}) async-start(), calls=%async_computation | async-start | bytes 6324224 | tf_op jit(solution)/shard_map/psum | solution.py:1000
  7.2 29.6 %collective-permute-start.27 = (bf16[2,256,2048]{2,1,0:T(8,128)(2,1)}, bf16[2,256,2048]{2,1,0:T(8,128)(2,1)}, u32[]{:S(2)}, u32[]{:S(2)}) collective-permute-start(bf16[2,256,2048]{2,1,0:T(8,128)(2,1)} %up_own.5), channel_id=1, source_target_pairs={{0,1},{1,0},{2,3},{3,2},{4,5},{5,4},{6,7},{7,6},{8,9},{9,8},{10,11... | collective-permute-start | bytes 6291464 | tf_op jit(solution)/shard_map/ppermute | solution.py:488
  7.8 29.1 %collective-permute-start.28 = (bf16[2,1024,512]{2,1,0:T(8,128)(2,1)}, bf16[2,1024,512]{2,1,0:T(8,128)(2,1)}, u32[]{:S(2)}, u32[]{:S(2)}) collective-permute-start(bf16[2,1024,512]{2,1,0:T(8,128)(2,1)} %down_own.5), channel_id=1, source_target_pairs={{0,1},{1,0},{2,3},{3,2},{4,5},{5,4},{6,7},{7,6},{8,9},{9,8},{10,11... | collective-permute-start | bytes 6291464 | tf_op jit(solution)/shard_map/ppermute | solution.py:488
  10.7 13.8 %collective-permute-start.23 = (bf16[2,12,256]{2,1,0:T(8,128)(2,1)S(1)}, bf16[2,12,256]{2,1,0:T(8,128)(2,1)S(1)}, u32[]{:S(2)}, u32[]{:S(2)}) collective-permute-start(bf16[2,12,256]{2,1,0:T(8,128)(2,1)S(1)} %concatenate.28), channel_id=1, source_target_pairs={{0,1},{1,0},{2,3},{3,2},{4,5},{5,4},{6,7},{7,6},{8,9},{9,8},{10,11... | collective-permute-start | bytes 36872 | tf_op jit(solution)/shard_map/ppermute | solution.py:488
  11.2 14.1 %collective-permute-start.25 = (bf16[2,256,1536]{2,1,0:T(8,128)(2,1)}, bf16[2,256,1536]{2,1,0:T(8,128)(2,1)}, u32[]{:S(2)}, u32[]{:S(2)}) collective-permute-start(bf16[2,256,1536]{2,1,0:T(8,128)(2,1)} %qkv_own.5), channel_id=1, source_target_pairs={{0,1},{1,0},{2,3},{3,2},{4,5},{5,4},{6,7},{7,6},{8,9},{9,8},{10,11... | collective-permute-start | bytes 4718600 | tf_op jit(solution)/shard_map/ppermute | solution.py:488
  17.4 7.8 %collective-permute-start.26 = (bf16[2,256,512]{2,1,0:T(8,128)(2,1)}, bf16[2,256,512]{2,1,0:T(8,128)(2,1)}, u32[]{:S(2)}, u32[]{:S(2)}) collective-permute-start(bf16[2,256,512]{2,1,0:T(8,128)(2,1)} %proj_own.5), channel_id=1, source_target_pairs={{0,1},{1,0},{2,3},{3,2},{4,5},{5,4},{6,7},{7,6},{8,9},{9,8},{10,11... | collective-permute-start | bytes 1572872 | tf_op jit(solution)/shard_map/ppermute | solution.py:488
  69.4 18.4 %collective-permute-start.29 = (bf16[2048,512]{1,0:T(8,128)(2,1)S(1)}, bf16[2048,512]{1,0:T(8,128)(2,1)S(1)}, u32[]{:S(2)}, u32[]{:S(2)}) collective-permute-start(bf16[2048,512]{1,0:T(8,128)(2,1)S(1)} %get-tuple-element.234), channel_id=1, source_target_pairs={{0,1},{1,0},{2,3},{3,2},{4,5},{5,4},{6,7},{7,6},{8,9},{9,8},{10,11... | collective-permute-start | bytes 6291464 | tf_op jit(solution)/shard_map/ppermute | solution.py:488
  114.0 20.9 %collective-permute-start.1 = (bf16[512,512]{1,0:T(8,128)(2,1)S(1)}, bf16[512,512]{1,0:T(8,128)(2,1)S(1)}, u32[]{:S(2)}, u32[]{:S(2)}) collective-permute-start(bf16[512,512]{1,0:T(8,128)(2,1)S(1)} %get-tuple-element.74), channel_id=1, source_target_pairs={{0,2},{2,0},{4,6},{6,4},{8,10},{10,8},{12,14},{14,12},{16,18},{18,... | collective-permute-start | bytes 1572872 | tf_op jit(solution)/shard_map/cond/branch_1_fun/ppermute | solution.py:497
  117.4 17.5 %collective-permute-start.2 = (bf16[512,512]{1,0:T(8,128)(2,1)S(1)}, bf16[512,512]{1,0:T(8,128)(2,1)S(1)}, u32[]{:S(2)}, u32[]{:S(2)}) collective-permute-start(bf16[512,512]{1,0:T(8,128)(2,1)S(1)} %get-tuple-element.96), channel_id=1, source_target_pairs={{0,4},{2,6},{4,0},{6,2},{8,12},{10,14},{12,8},{14,10},{16,20},{18,... | collective-permute-start | bytes 1572872 | tf_op jit(solution)/shard_map/cond/branch_1_fun/ppermute | solution.py:497
  135.7 16.5 %collective-permute-start.3 = (bf16[1024,512]{1,0:T(8,128)(2,1)}, bf16[1024,512]{1,0:T(8,128)(2,1)}, u32[]{:S(2)}, u32[]{:S(2)}) collective-permute-start(bf16[1024,512]{1,0:T(8,128)(2,1)} %get-tuple-element.103), channel_id=1, source_target_pairs={{0,1},{1,0},{2,3},{3,2},{4,5},{5,4},{6,7},{7,6},{8,9},{9,8},{10,11... | collective-permute-start | bytes 3145736 | tf_op jit(solution)/shard_map/cond/branch_1_fun/ppermute | solution.py:488
  154.6 15.1 %collective-permute-start.7 = (bf16[288,512]{1,0:T(8,128)(2,1)S(1)}, bf16[288,512]{1,0:T(8,128)(2,1)S(1)}, u32[]{:S(2)}, u32[]{:S(2)}) collective-permute-start(bf16[288,512]{1,0:T(8,128)(2,1)S(1)} %get-tuple-element.123), channel_id=1, source_target_pairs={{0,2},{2,0},{4,6},{6,4},{8,10},{10,8},{12,14},{14,12},{16,18},{18,... | collective-permute-start | bytes 884744 | tf_op jit(solution)/shard_map/cond/branch_1_fun/ppermute | solution.py:497
  155.1 14.6 %collective-permute-start.8 = (bf16[288,512]{1,0:T(8,128)(2,1)S(1)}, bf16[288,512]{1,0:T(8,128)(2,1)S(1)}, u32[]{:S(2)}, u32[]{:S(2)}) collective-permute-start(bf16[288,512]{1,0:T(8,128)(2,1)S(1)} %get-tuple-element.125), channel_id=1, source_target_pairs={{0,4},{2,6},{4,0},{6,2},{8,12},{10,14},{12,8},{14,10},{16,20},{18,... | collective-permute-start | bytes 884744 | tf_op jit(solution)/shard_map/cond/branch_1_fun/ppermute | solution.py:497
  156.3 13.4 %collective-permute-start.5 = (bf16[256,512]{1,0:T(8,128)(2,1)S(1)}, bf16[256,512]{1,0:T(8,128)(2,1)S(1)}, u32[]{:S(2)}, u32[]{:S(2)}) collective-permute-start(bf16[256,512]{1,0:T(8,128)(2,1)S(1)} %get-tuple-element.118), channel_id=1, source_target_pairs={{0,4},{2,6},{4,0},{6,2},{8,12},{10,14},{12,8},{14,10},{16,20},{18,... | collective-permute-start | bytes 786440 | tf_op jit(solution)/shard_map/cond/branch_1_fun/ppermute | solution.py:497
  157.1 12.6 %collective-permute-start.6 = (bf16[256,512]{1,0:T(8,128)(2,1)S(1)}, bf16[256,512]{1,0:T(8,128)(2,1)S(1)}, u32[]{:S(2)}, u32[]{:S(2)}) collective-permute-start(bf16[256,512]{1,0:T(8,128)(2,1)S(1)} %get-tuple-element.121), channel_id=1, source_target_pairs={{0,2},{2,0},{4,6},{6,4},{8,10},{10,8},{12,14},{14,12},{16,18},{18,... | collective-permute-start | bytes 786440 | tf_op jit(solution)/shard_map/cond/branch_1_fun/ppermute | solution.py:497
  170.5 16.4 %collective-permute-start.9 = (bf16[512,512]{1,0:T(8,128)(2,1)S(1)}, bf16[512,512]{1,0:T(8,128)(2,1)S(1)}, u32[]{:S(2)}, u32[]{:S(2)}) collective-permute-start(bf16[512,512]{1,0:T(8,128)(2,1)S(1)} %get-tuple-element.139.refs_0_), channel_id=1, source_target_pairs={{0,8},{2,10},{4,12},{6,14},{8,0},{10,2},{12,4},{14,6},{16,24},{18,... | collective-permute-start | bytes 1572872 | tf_op jit(solution)/shard_map/cond/branch_1_fun/ppermute | solution.py:497
  187.7 31.4 %collective-permute-start.12 = (bf16[512,512]{1,0:T(8,128)(2,1)S(1)}, bf16[512,512]{1,0:T(8,128)(2,1)S(1)}, u32[]{:S(2)}, u32[]{:S(2)}) collective-permute-start(bf16[512,512]{1,0:T(8,128)(2,1)S(1)} %get-tuple-element.147.refs_0_), channel_id=1, source_target_pairs={{0,16},{2,18},{4,20},{6,22},{8,24},{10,26},{12,28},{14,30},{16,0},... | collective-permute-start | bytes 1572872 | tf_op jit(solution)/shard_map/cond/branch_1_fun/ppermute | solution.py:497
  190.5 22.9 %collective-permute-start.13 = (bf16[288,512]{1,0:T(8,128)(2,1)S(1)}, bf16[288,512]{1,0:T(8,128)(2,1)S(1)}, u32[]{:S(2)}, u32[]{:S(2)}) collective-permute-start(bf16[288,512]{1,0:T(8,128)(2,1)S(1)} %get-tuple-element.149.refs_2_), channel_id=1, source_target_pairs={{0,8},{2,10},{4,12},{6,14},{8,0},{10,2},{12,4},{14,6},{16,24},{18,... | collective-permute-start | bytes 884744 | tf_op jit(solution)/shard_map/cond/branch_1_fun/ppermute | solution.py:497
  220.6 38.2 %collective-permute-start.14 = (bf16[512,512]{1,0:T(8,128)(2,1)}, bf16[512,512]{1,0:T(8,128)(2,1)}, u32[]{:S(2)}, u32[]{:S(2)}) collective-permute-start(bf16[512,512]{1,0:T(8,128)(2,1)} %get-tuple-element.426), channel_id=1, source_target_pairs={{0,2},{2,0},{4,6},{6,4},{8,10},{10,8},{12,14},{14,12},{16,18},{18,... | collective-permute-start | bytes 1572872 | tf_op jit(solution)/shard_map/cond/branch_1_fun/ppermute | solution.py:497
  222.0 36.7 %collective-permute-start.15 = (bf16[512,512]{1,0:T(8,128)(2,1)}, bf16[512,512]{1,0:T(8,128)(2,1)}, u32[]{:S(2)}, u32[]{:S(2)}) collective-permute-start(bf16[512,512]{1,0:T(8,128)(2,1)} %get-tuple-element.426), channel_id=1, source_target_pairs={{0,4},{2,6},{4,0},{6,2},{8,12},{10,14},{12,8},{14,10},{16,20},{18,... | collective-permute-start | bytes 1572872 | tf_op jit(solution)/shard_map/cond/branch_1_fun/ppermute | solution.py:497
  222.1 33.6 %collective-permute-start.18 = (bf16[288,512]{1,0:T(8,128)(2,1)S(1)}, bf16[288,512]{1,0:T(8,128)(2,1)S(1)}, u32[]{:S(2)}, u32[]{:S(2)}) collective-permute-start(bf16[288,512]{1,0:T(8,128)(2,1)S(1)} %get-tuple-element.156.refs_0_), channel_id=1, source_target_pairs={{0,16},{2,18},{4,20},{6,22},{8,24},{10,26},{12,28},{14,30},{16,0},... | collective-permute-start | bytes 884744 | tf_op jit(solution)/shard_map/cond/branch_1_fun/ppermute | solution.py:497
  257.0 9.9 %collective-permute-start.19 = (bf16[288,512]{1,0:T(8,128)(2,1)}, bf16[288,512]{1,0:T(8,128)(2,1)}, u32[]{:S(2)}, u32[]{:S(2)}) collective-permute-start(bf16[288,512]{1,0:T(8,128)(2,1)} %reduce_step.11), channel_id=1, source_target_pairs={{0,2},{2,0},{4,6},{6,4},{8,10},{10,8},{12,14},{14,12},{16,18},{18,... | collective-permute-start | bytes 884744 | tf_op jit(solution)/shard_map/cond/branch_1_fun/ppermute | solution.py:497
  257.1 10.3 %collective-permute-start.20 = (bf16[288,512]{1,0:T(8,128)(2,1)}, bf16[288,512]{1,0:T(8,128)(2,1)}, u32[]{:S(2)}, u32[]{:S(2)}) collective-permute-start(bf16[288,512]{1,0:T(8,128)(2,1)} %reduce_step.11), channel_id=1, source_target_pairs={{0,4},{2,6},{4,0},{6,2},{8,12},{10,14},{12,8},{14,10},{16,20},{18,... | collective-permute-start | bytes 884744 | tf_op jit(solution)/shard_map/cond/branch_1_fun/ppermute | solution.py:497
  259.7 16.5 %collective-permute-start.16 = (bf16[256,512]{1,0:T(8,128)(2,1)S(1)}, bf16[256,512]{1,0:T(8,128)(2,1)}, u32[]{:S(2)}, u32[]{:S(2)}) collective-permute-start(bf16[256,512]{1,0:T(8,128)(2,1)S(1)} %slice.46), channel_id=1, source_target_pairs={{0,4},{2,6},{4,0},{6,2},{8,12},{10,14},{12,8},{14,10},{16,20},{18,... | collective-permute-start | bytes 786440 | tf_op jit(solution)/shard_map/cond/branch_1_fun/ppermute | solution.py:497
  261.2 15.0 %collective-permute-start.17 = (bf16[256,512]{1,0:T(8,128)(2,1)S(1)}, bf16[256,512]{1,0:T(8,128)(2,1)}, u32[]{:S(2)}, u32[]{:S(2)}) collective-permute-start(bf16[256,512]{1,0:T(8,128)(2,1)S(1)} %slice.47), channel_id=1, source_target_pairs={{0,2},{2,0},{4,6},{6,4},{8,10},{10,8},{12,14},{14,12},{16,18},{18,... | collective-permute-start | bytes 786440 | tf_op jit(solution)/shard_map/cond/branch_1_fun/ppermute | solution.py:497
  (45 other events, 253.8 us)
Sparse Core Ops, SparseCore 0:
  90.4 170.5 all-reduce.7

commit v2 on v1

--- a/solution.py
+++ b/solution.py
@@ -866,7 +866,7 @@
 
     def table_rows(pairs):
         flat = (
-            pairs.reshape(2, QUADS, ROWS, 4, ROWS).transpose(0, 1, 3, 2, 4).reshape(2 * HEADS, -1)
+            pairs.reshape(QUADS, ROWS, 4, ROWS).transpose(0, 2, 1, 3).reshape(HEADS, -1)
         )
         heads = jnp.einsum("hp,rp->hr", flat, onehot_f, precision=lax.Precision.HIGH)
         return jnp.pad(heads, ((0, 0), (0, D - LIVE)))
@@ -972,7 +972,7 @@
         attn_got = swap_cores(attn_send)
         tiny = [attn_sums, mlp_sums]
         if layer == 0:
-            tiny.append(table_rows(jnp.stack([pairs, pairs_upper])))
+            tiny += [table_rows(pairs), table_rows(pairs_upper)]
         tiny = jnp.concatenate(tiny, axis=0).astype(bf16)
         tiny_got = swap_cores(tiny)
         if layer == 1:

time: 293 us -> 299 us (1.020)
  local copies, waits for them, and re-layouts: 38 us -> 43.3 us
    reshape x1 -> x6, local copies, waits for them, and re-layouts: 2.38 us -> 11.6 us  [table_rows(): pairs.reshape(QUADS, ROWS, 4, ROWS).transpose(0, 2, 1, 3).reshape(HEADS, -1)]
    another operation x5 -> x1, local copies, waits for them, and re-layouts: 7.01 us -> 0.04 us  [the longest x4 6.96 us: backward(): tiny.append(table_rows(jnp.stack([pairs, pairs_upper])))]
    dot_general x1 -> x2, matrix products: 3.44 us -> 6.3 us  [table_rows(): jnp.einsum('hp,rp->hr', flat, onehot_f, precision=lax.Precision.HIGH)]
  transfers between devices with their start and end apart: 33 -> 33, of which waited for: 12 -> 14; matrix products, arithmetic and copies ran while one was open for 14% -> 16% of each run, Pallas kernels for 21% -> 21%
where the time goes in v2:
time: 299 us; the launch traced here: 298 us
  Pallas kernels  103 us (34%)
  waiting for transfers between devices  97.5 us (33%)
  local copies, waits for them, and re-layouts  43.3 us (14%)
  starting transfers between devices  29.6 us (10%)
  between operations  14.5 us (5%)
  matrix products  6.9 us (2%)
  other arithmetic  3 us (1%)
    ppermute x20, waiting for transfers between devices, dp_swap(): lax.ppermute(value, 'dp', [(at, at ^ 1 << bit) for at in range(count)])  90.6 us
    pallas_call x8, Pallas kernels, call(): pl.pallas_call(functools.partial(kernel, layer, rows), in_specs=[pl.Block...  87.5 us
    ppermute x20, starting transfers between devices, dp_swap(): lax.ppermute(value, 'dp', [(at, at ^ 1 << bit) for at in range(count)])  26 us
    reshape x6, local copies, waits for them, and re-layouts, table_rows(): pairs.reshape(QUADS, ROWS, 4, ROWS).transpose(0, 2, 1, 3).reshape(HEADS, -1)  11.6 us
    ppermute x12, waiting for transfers between devices, swap_cores(): return lax.ppermute(value, 'fsdp', [(0, 1), (1, 0)])  6.8 us
    pallas_call x1, Pallas kernels, body(): pl.pallas_call(unpack_kernel, in_specs=[pl.BlockSpec(memory_space=pltpu.S...  6.73 us
    pallas_call x6, Pallas kernels, advance(): pl.pallas_call(functools.partial(step_kernel, plan), in_specs=[pl.BlockSp...  6.39 us
    dot_general x2, matrix products, table_rows(): jnp.einsum('hp,rp->hr', flat, onehot_f, precision=lax.Precision.HIGH)  6.3 us
  transfers between devices with their start and end apart: 33, of which 14 were waited for; matrix products, arithmetic and copies ran while one was open for 16% of the time, Pallas kernels for 21%

profile of v2, /device:TPU:0, one launch (start us, length us, event | category | flops | bytes accessed | tf_op | source)
XLA Modules:
  0.0 298.1 jit_solution(13302380890020334077)
XLA Ops:
  22.0 3.0 %copy.76 = f32[2,4,4,64,64]{4,2,3,1,0:T(4,128)} copy(f32[2,4,4,64,64]{4,3,2,1,0:T(8,128)} %reshape.134) | data formatting | bytes 1048576 | tf_op jit(solution)/shard_map/reshape | solution.py:790
  28.4 11.5 %attention_forward_kernel0.1 = (f32[512,512]{1,0:T(8,128)S(1)}, bf16[512,512]{1,0:T(8,128)(2,1)}, bf16[512,1536]{1,0:T(8,128)(2,1)}, f32[8,4,64,256]{3,2,1,0:T(8,128)}, bf16[512,512]{1,0:T(8,128)(2,1)}) custom-call(s32[1]{0:T(128)} %bitcast.20.core_ref, bf16[2,196,512]{2,1,0:T(8,128)(2,1)S(1)} %copy.60.source, bf16[256,196]{1,0:T(8,128)(2,1)S(1)} %copy-done.11, ...), custom_call_target="tpu_custom_call" | custom-call | flops 1 | bytes 1 | tf_op jit(solution)/shard_map/attention_forward_kernel0/pallas_call | solution.py:470
  40.0 7.3 %mlp_forward_kernel0.1 = (f32[512,512]{1,0:T(8,128)S(1)}, bf16[512,512]{1,0:T(8,128)(2,1)}, bf16[512,2048]{1,0:T(8,128)(2,1)}, bf16[512,2048]{1,0:T(8,128)(2,1)}) custom-call(s32[1]{0:T(128)} %bitcast.20.core_ref, f32[512,512]{1,0:T(8,128)S(1)} %get-tuple-element.226.middle, f32[16,512]{1,0:T(8,128)S(1)} %get-tuple-element.408.small, ...), custom_call_target="tpu_custom_call" | custom-call | flops 1 | bytes 1 | tf_op jit(solution)/shard_map/mlp_forward_kernel0/pallas_call | solution.py:470
  47.3 8.8 %attention_forward_kernel1.1 = (f32[512,512]{1,0:T(8,128)S(1)}, bf16[512,512]{1,0:T(8,128)(2,1)S(1)}, bf16[512,1536]{1,0:T(8,128)(2,1)S(1)}, f32[8,4,64,256]{3,2,1,0:T(8,128)S(1)}, bf16[512,512]{1,0:T(8,128)(2,1)S(1)}) custom-call(s32[1]{0:T(128)} %bitcast.20.core_ref, f32[512,512]{1,0:T(8,128)S(1)} %get-tuple-element.227.source, ...), custom_call_target="tpu_custom_call" | custom-call | flops 1 | bytes 1 | tf_op jit(solution)/shard_map/attention_forward_kernel1/pallas_call | solution.py:470
  56.2 6.1 %mlp_forward_kernel1.1 = (f32[512,512]{1,0:T(8,128)S(1)}, bf16[512,512]{1,0:T(8,128)(2,1)S(1)}, bf16[512,2048]{1,0:T(8,128)(2,1)S(1)}, bf16[512,2048]{1,0:T(8,128)(2,1)S(1)}) custom-call(s32[1]{0:T(128)} %bitcast.20.core_ref, f32[512,512]{1,0:T(8,128)S(1)} %get-tuple-element.228.middle, f32[16,512]{1,0:T(8,128)S(1)} %get-tuple-element.407.small, ...), custom_call_target="tpu_custom_call" | custom-call | flops 1 | bytes 1 | tf_op jit(solution)/shard_map/mlp_forward_kernel1/pallas_call | solution.py:470
  62.3 10.2 %mlp_backward_kernel1.1 = (f32[512,512]{1,0:T(8,128)S(1)}, f32[8,512]{1,0:T(8,128)S(1)}, bf16[2048,512]{1,0:T(8,128)(2,1)S(1)}, bf16[2048,512]{1,0:T(8,128)(2,1)S(1)}) custom-call(s32[1]{0:T(128)} %bitcast.20.core_ref, bf16[2,196,512]{2,1,0:T(8,128)(2,1)S(1)} %copy.63.grad, bf16[256,196]{1,0:T(8,128)(2,1)S(1)} %copy-done.12, ...), custom_call_target="tpu_custom_call" | custom-call | flops 1 | bytes 1 | tf_op jit(solution)/shard_map/mlp_backward_kernel1/pallas_call | solution.py:470
  73.0 15.1 %attention_backward_kernel1.1 = (f32[512,512]{1,0:T(8,128)}, f32[8,512]{1,0:T(8,128)S(1)}, f32[4,64,256]{2,1,0:T(8,128)}, bf16[1024,512]{1,0:T(8,128)(2,1)S(1)}, bf16[1024,512]{1,0:T(8,128)(2,1)S(1)}) custom-call(s32[1]{0:T(128)} %bitcast.20.core_ref, f32[512,512]{1,0:T(8,128)S(1)} %get-tuple-element.235.middle_grad, ...), custom_call_target="tpu_custom_call" | custom-call | flops 1 | bytes 1 | tf_op jit(solution)/shard_map/attention_backward_kernel1/pallas_call | solution.py:470
  90.9 2.4 merge.1
  98.3 183.7 %conditional.1 = (bf16[512,512]{1,0:T(8,128)(2,1)}, bf16[512,512]{1,0:T(8,128)(2,1)}, bf16[512,512]{1,0:T(8,128)(2,1)}, bf16[256,512]{1,0:T(8,128)(2,1)}, bf16[2...) conditional(s32[]{:T(128)} %convert_element_type.27, () %tuple.27, ...), branch_computations={%region_0.1_spmd, %region_1.2_spmd} | conditional | flops 138769920 | bytes 104914472 | solution.py:1002
  98.3 13.3 %mlp_backward_kernel0.1 = (f32[512,512]{1,0:T(8,128)S(1)}, f32[8,512]{1,0:T(8,128)S(1)}, bf16[2048,512]{1,0:T(8,128)(2,1)S(1)}, bf16[2048,512]{1,0:T(8,128)(2,1)S(1)}) custom-call(s32[1]{0:T(128)} %get-tuple-element.54.core_ref, f32[512,512]{1,0:T(8,128)S(1)} %get-tuple-element.56.grad, bf16[256,196]{1,0:T(8,128)(2,1)S(1)} %get-tuple-element.57.lay, ...), custom_call_target="tpu_custom_call" | custom-call | flops 1 | bytes 1 | tf_op jit(solution)/shard_map/cond/branch_1_fun/mlp_backward_kernel0/pallas_call | solution.py:470
  112.0 3.9 %collective-permute-done = bf16[2048,512]{1,0:T(8,128)(2,1)S(1)} collective-permute-done((bf16[2048,512]{1,0:T(8,128)(2,1)S(1)}, bf16[2048,512]{1,0:T(8,128)(2,1)S(1)}, u32[]{:S(2)}, u32[]{:S(2)}) %collective-permute-start) | collective-permute-done | bytes 2097184 | tf_op jit(solution)/shard_map/cond/branch_1_fun/ppermute | solution.py:488
  117.2 3.4 %collective-permute-start.1 = (bf16[512,512]{1,0:T(8,128)(2,1)S(1)}, bf16[512,512]{1,0:T(8,128)(2,1)S(1)}, u32[]{:S(2)}, u32[]{:S(2)}) collective-permute-start(bf16[512,512]{1,0:T(8,128)(2,1)S(1)} %get-tuple-element.74), channel_id=1, source_target_pairs={{0,2},{2,0},{4,6},{6,4},{8,10},{10,8},{12,14},{14,12},{16,18},{18,... | collective-permute-start | bytes 1572872 | tf_op jit(solution)/shard_map/cond/branch_1_fun/ppermute | solution.py:497
  122.2 15.1 %attention_backward_kernel0.1 = (f32[2,196,512]{2,1,0:T(8,128)S(1)}, f32[8,512]{1,0:T(8,128)S(1)}, f32[4,64,256]{2,1,0:T(8,128)S(1)}, bf16[1024,512]{1,0:T(8,128)(2,1)S(1)}, bf16[1024,512]{1,0:T(8,128)(2,1)}) custom-call(s32[1]{0:T(128)} %get-tuple-element.54.core_ref, f32[512,512]{1,0:T(8,128)S(1)} %get-tuple-element.76.middle_grad, ...), custom_call_target="tpu_custom_call" | custom-call | flops 1 | bytes 1 | tf_op jit(solution)/shard_map/cond/branch_1_fun/attention_backward_kernel0/pallas_call | solution.py:470
  144.7 3.2 %convolution_convert_fusion = bf16[16,176]{1,0:T(8,128)(2,1)S(1)} fusion(f32[16,4096]{1,0:T(8,128)} %reshape.113, f32[176,4096]{1,0:T(8,128)} %get-tuple-element.106), kind=kOutput, calls=%fused_computation | convolution fusion | flops 69208832 | bytes 3151360 | tf_op jit(solution)/shard_map/cond/branch_1_fun/hp,rp->hr/dot_general | solution.py:871
  153.6 3.1 %convolution_convert_fusion.1 = bf16[16,176]{1,0:T(8,128)(2,1)S(1)} fusion(f32[16,4096]{1,0:T(8,128)} %reshape.111, f32[176,4096]{1,0:T(8,128)} %get-tuple-element.106), kind=kOutput, calls=%fused_computation.1 | convolution fusion | flops 69208832 | bytes 3151360 | tf_op jit(solution)/shard_map/cond/branch_1_fun/hp,rp->hr/dot_general | solution.py:871
  164.8 11.1 %collective-permute-done.5.refs_1_ = bf16[256,512]{1,0:T(8,128)(2,1)S(1)} collective-permute-done((bf16[256,512]{1,0:T(8,128)(2,1)S(1)}, bf16[256,512]{1,0:T(8,128)(2,1)S(1)}, u32[]{:S(2)}, u32[]{:S(2)}) %collective-permute-start.5) | collective-permute-done | bytes 262176 | tf_op jit(solution)/shard_map/cond/branch_1_fun/ppermute | solution.py:497
  180.3 3.1 %collective-permute-done.10.refs_3_ = bf16[144,512]{1,0:T(8,128)(2,1)S(1)} collective-permute-done((bf16[144,512]{1,0:T(8,128)(2,1)S(1)}, bf16[144,512]{1,0:T(8,128)(2,1)S(1)}, u32[]{:S(2)}, u32[]{:S(2)}) %collective-permute-start.10) | collective-permute-done | bytes 147488 | tf_op jit(solution)/shard_map/cond/branch_1_fun/ppermute | solution.py:497
  184.4 8.1 %collective-permute-done.9.refs_1_ = bf16[512,512]{1,0:T(8,128)(2,1)S(1)} collective-permute-done((bf16[512,512]{1,0:T(8,128)(2,1)S(1)}, bf16[512,512]{1,0:T(8,128)(2,1)S(1)}, u32[]{:S(2)}, u32[]{:S(2)}) %collective-permute-start.9) | collective-permute-done | bytes 524320 | tf_op jit(solution)/shard_map/cond/branch_1_fun/ppermute | solution.py:497
  193.3 2.6 collective-permute-start.12
  197.0 22.0 %collective-permute-done.13.refs_3_ = bf16[288,512]{1,0:T(8,128)(2,1)S(1)} collective-permute-done((bf16[288,512]{1,0:T(8,128)(2,1)S(1)}, bf16[288,512]{1,0:T(8,128)(2,1)S(1)}, u32[]{:S(2)}, u32[]{:S(2)}) %collective-permute-start.13) | collective-permute-done | bytes 294944 | tf_op jit(solution)/shard_map/cond/branch_1_fun/ppermute | solution.py:497
  219.0 6.2 %collective-permute-done.12.refs_1_ = bf16[512,512]{1,0:T(8,128)(2,1)S(1)} collective-permute-done((bf16[512,512]{1,0:T(8,128)(2,1)S(1)}, bf16[512,512]{1,0:T(8,128)(2,1)S(1)}, u32[]{:S(2)}, u32[]{:S(2)}) %collective-permute-start.12) | collective-permute-done | bytes 524320 | tf_op jit(solution)/shard_map/cond/branch_1_fun/ppermute | solution.py:497
  228.6 33.0 %collective-permute-done.18.refs_1_ = bf16[288,512]{1,0:T(8,128)(2,1)S(1)} collective-permute-done((bf16[288,512]{1,0:T(8,128)(2,1)S(1)}, bf16[288,512]{1,0:T(8,128)(2,1)S(1)}, u32[]{:S(2)}, u32[]{:S(2)}) %collective-permute-start.18) | collective-permute-done | bytes 294944 | tf_op jit(solution)/shard_map/cond/branch_1_fun/ppermute | solution.py:497
  269.0 4.1 %collective-permute-done.19 = bf16[288,512]{1,0:T(8,128)(2,1)} collective-permute-done((bf16[288,512]{1,0:T(8,128)(2,1)}, bf16[288,512]{1,0:T(8,128)(2,1)}, u32[]{:S(2)}, u32[]{:S(2)}) %collective-permute-start.19) | collective-permute-done | bytes 294944 | tf_op jit(solution)/shard_map/cond/branch_1_fun/ppermute | solution.py:497
  283.9 6.7 %unpack.1 = (f32[2,256,1536]{2,1,0:T(8,128)}, f32[2,256,512]{2,1,0:T(8,128)}, f32[2,256,2048]{2,1,0:T(8,128)}, f32[2,1024,512]{2,1,0:T(8,128)}, f32[2,2,256]{2,1...) custom-call(s32[3]{0:T(128)} %copy-done.37, ...), custom_call_target="tpu_custom_call" | custom-call | tf_op jit(solution)/shard_map/unpack/pallas_call | solution.py:1021
  (216 shorter events, 79.7 us)
Async XLA Ops:
  7.2 274.8 %all-reduce.9.cloned.1.call-start = ((), (), s32[]{:S(2)}) async-start(), calls=%async_computation | async-start | bytes 6324224 | tf_op jit(solution)/shard_map/psum | solution.py:1000
  7.2 32.7 %collective-permute-start.27 = (bf16[2,256,2048]{2,1,0:T(8,128)(2,1)}, bf16[2,256,2048]{2,1,0:T(8,128)(2,1)}, u32[]{:S(2)}, u32[]{:S(2)}) collective-permute-start(bf16[2,256,2048]{2,1,0:T(8,128)(2,1)} %up_own.5), channel_id=1, source_target_pairs={{0,1},{1,0},{2,3},{3,2},{4,5},{5,4},{6,7},{7,6},{8,9},{9,8},{10,11... | collective-permute-start | bytes 6291464 | tf_op jit(solution)/shard_map/ppermute | solution.py:488
  7.8 32.2 %collective-permute-start.28 = (bf16[2,1024,512]{2,1,0:T(8,128)(2,1)}, bf16[2,1024,512]{2,1,0:T(8,128)(2,1)}, u32[]{:S(2)}, u32[]{:S(2)}) collective-permute-start(bf16[2,1024,512]{2,1,0:T(8,128)(2,1)} %down_own.5), channel_id=1, source_target_pairs={{0,1},{1,0},{2,3},{3,2},{4,5},{5,4},{6,7},{7,6},{8,9},{9,8},{10,11... | collective-permute-start | bytes 6291464 | tf_op jit(solution)/shard_map/ppermute | solution.py:488
  11.9 14.9 %collective-permute-start.23 = (bf16[2,12,256]{2,1,0:T(8,128)(2,1)}, bf16[2,12,256]{2,1,0:T(8,128)(2,1)}, u32[]{:S(2)}, u32[]{:S(2)}) collective-permute-start(bf16[2,12,256]{2,1,0:T(8,128)(2,1)} %concatenate.27), channel_id=1, source_target_pairs={{0,1},{1,0},{2,3},{3,2},{4,5},{5,4},{6,7},{7,6},{8,9},{9,8},{10,11... | collective-permute-start | bytes 36872 | tf_op jit(solution)/shard_map/ppermute | solution.py:488
  12.4 16.0 %collective-permute-start.25 = (bf16[2,256,1536]{2,1,0:T(8,128)(2,1)}, bf16[2,256,1536]{2,1,0:T(8,128)(2,1)}, u32[]{:S(2)}, u32[]{:S(2)}) collective-permute-start(bf16[2,256,1536]{2,1,0:T(8,128)(2,1)} %qkv_own.5), channel_id=1, source_target_pairs={{0,1},{1,0},{2,3},{3,2},{4,5},{5,4},{6,7},{7,6},{8,9},{9,8},{10,11... | collective-permute-start | bytes 4718600 | tf_op jit(solution)/shard_map/ppermute | solution.py:488
  19.8 8.6 %collective-permute-start.26 = (bf16[2,256,512]{2,1,0:T(8,128)(2,1)}, bf16[2,256,512]{2,1,0:T(8,128)(2,1)}, u32[]{:S(2)}, u32[]{:S(2)}) collective-permute-start(bf16[2,256,512]{2,1,0:T(8,128)(2,1)} %proj_own.5), channel_id=1, source_target_pairs={{0,1},{1,0},{2,3},{3,2},{4,5},{5,4},{6,7},{7,6},{8,9},{9,8},{10,11... | collective-permute-start | bytes 1572872 | tf_op jit(solution)/shard_map/ppermute | solution.py:488
  72.5 18.4 %collective-permute-start.29 = (bf16[2048,512]{1,0:T(8,128)(2,1)S(1)}, bf16[2048,512]{1,0:T(8,128)(2,1)S(1)}, u32[]{:S(2)}, u32[]{:S(2)}) collective-permute-start(bf16[2048,512]{1,0:T(8,128)(2,1)S(1)} %get-tuple-element.234), channel_id=1, source_target_pairs={{0,1},{1,0},{2,3},{3,2},{4,5},{5,4},{6,7},{7,6},{8,9},{9,8},{10,11... | collective-permute-start | bytes 6291464 | tf_op jit(solution)/shard_map/ppermute | solution.py:488
  117.2 20.9 %collective-permute-start.1 = (bf16[512,512]{1,0:T(8,128)(2,1)S(1)}, bf16[512,512]{1,0:T(8,128)(2,1)S(1)}, u32[]{:S(2)}, u32[]{:S(2)}) collective-permute-start(bf16[512,512]{1,0:T(8,128)(2,1)S(1)} %get-tuple-element.74), channel_id=1, source_target_pairs={{0,2},{2,0},{4,6},{6,4},{8,10},{10,8},{12,14},{14,12},{16,18},{18,... | collective-permute-start | bytes 1572872 | tf_op jit(solution)/shard_map/cond/branch_1_fun/ppermute | solution.py:497
  120.6 17.5 %collective-permute-start.2 = (bf16[512,512]{1,0:T(8,128)(2,1)S(1)}, bf16[512,512]{1,0:T(8,128)(2,1)S(1)}, u32[]{:S(2)}, u32[]{:S(2)}) collective-permute-start(bf16[512,512]{1,0:T(8,128)(2,1)S(1)} %get-tuple-element.96), channel_id=1, source_target_pairs={{0,4},{2,6},{4,0},{6,2},{8,12},{10,14},{12,8},{14,10},{16,20},{18,... | collective-permute-start | bytes 1572872 | tf_op jit(solution)/shard_map/cond/branch_1_fun/ppermute | solution.py:497
  138.9 19.4 %collective-permute-start.3 = (bf16[1024,512]{1,0:T(8,128)(2,1)}, bf16[1024,512]{1,0:T(8,128)(2,1)}, u32[]{:S(2)}, u32[]{:S(2)}) collective-permute-start(bf16[1024,512]{1,0:T(8,128)(2,1)} %get-tuple-element.103), channel_id=1, source_target_pairs={{0,1},{1,0},{2,3},{3,2},{4,5},{5,4},{6,7},{7,6},{8,9},{9,8},{10,11... | collective-permute-start | bytes 3145736 | tf_op jit(solution)/shard_map/cond/branch_1_fun/ppermute | solution.py:488
  160.7 15.2 %collective-permute-start.7 = (bf16[288,512]{1,0:T(8,128)(2,1)S(1)}, bf16[288,512]{1,0:T(8,128)(2,1)S(1)}, u32[]{:S(2)}, u32[]{:S(2)}) collective-permute-start(bf16[288,512]{1,0:T(8,128)(2,1)S(1)} %get-tuple-element.123), channel_id=1, source_target_pairs={{0,2},{2,0},{4,6},{6,4},{8,10},{10,8},{12,14},{14,12},{16,18},{18,... | collective-permute-start | bytes 884744 | tf_op jit(solution)/shard_map/cond/branch_1_fun/ppermute | solution.py:497
  161.2 14.6 %collective-permute-start.8 = (bf16[288,512]{1,0:T(8,128)(2,1)S(1)}, bf16[288,512]{1,0:T(8,128)(2,1)S(1)}, u32[]{:S(2)}, u32[]{:S(2)}) collective-permute-start(bf16[288,512]{1,0:T(8,128)(2,1)S(1)} %get-tuple-element.125), channel_id=1, source_target_pairs={{0,4},{2,6},{4,0},{6,2},{8,12},{10,14},{12,8},{14,10},{16,20},{18,... | collective-permute-start | bytes 884744 | tf_op jit(solution)/shard_map/cond/branch_1_fun/ppermute | solution.py:497
  162.5 13.3 %collective-permute-start.5 = (bf16[256,512]{1,0:T(8,128)(2,1)S(1)}, bf16[256,512]{1,0:T(8,128)(2,1)S(1)}, u32[]{:S(2)}, u32[]{:S(2)}) collective-permute-start(bf16[256,512]{1,0:T(8,128)(2,1)S(1)} %get-tuple-element.118), channel_id=1, source_target_pairs={{0,4},{2,6},{4,0},{6,2},{8,12},{10,14},{12,8},{14,10},{16,20},{18,... | collective-permute-start | bytes 786440 | tf_op jit(solution)/shard_map/cond/branch_1_fun/ppermute | solution.py:497
  163.3 12.6 %collective-permute-start.6 = (bf16[256,512]{1,0:T(8,128)(2,1)S(1)}, bf16[256,512]{1,0:T(8,128)(2,1)S(1)}, u32[]{:S(2)}, u32[]{:S(2)}) collective-permute-start(bf16[256,512]{1,0:T(8,128)(2,1)S(1)} %get-tuple-element.121), channel_id=1, source_target_pairs={{0,2},{2,0},{4,6},{6,4},{8,10},{10,8},{12,14},{14,12},{16,18},{18,... | collective-permute-start | bytes 786440 | tf_op jit(solution)/shard_map/cond/branch_1_fun/ppermute | solution.py:497
  176.7 15.9 %collective-permute-start.9 = (bf16[512,512]{1,0:T(8,128)(2,1)S(1)}, bf16[512,512]{1,0:T(8,128)(2,1)S(1)}, u32[]{:S(2)}, u32[]{:S(2)}) collective-permute-start(bf16[512,512]{1,0:T(8,128)(2,1)S(1)} %get-tuple-element.139.refs_0_), channel_id=1, source_target_pairs={{0,8},{2,10},{4,12},{6,14},{8,0},{10,2},{12,4},{14,6},{16,24},{18,... | collective-permute-start | bytes 1572872 | tf_op jit(solution)/shard_map/cond/branch_1_fun/ppermute | solution.py:497
  193.3 31.9 %collective-permute-start.12 = (bf16[512,512]{1,0:T(8,128)(2,1)S(1)}, bf16[512,512]{1,0:T(8,128)(2,1)S(1)}, u32[]{:S(2)}, u32[]{:S(2)}) collective-permute-start(bf16[512,512]{1,0:T(8,128)(2,1)S(1)} %get-tuple-element.147.refs_0_), channel_id=1, source_target_pairs={{0,16},{2,18},{4,20},{6,22},{8,24},{10,26},{12,28},{14,30},{16,0},... | collective-permute-start | bytes 1572872 | tf_op jit(solution)/shard_map/cond/branch_1_fun/ppermute | solution.py:497
  195.9 23.1 %collective-permute-start.13 = (bf16[288,512]{1,0:T(8,128)(2,1)S(1)}, bf16[288,512]{1,0:T(8,128)(2,1)S(1)}, u32[]{:S(2)}, u32[]{:S(2)}) collective-permute-start(bf16[288,512]{1,0:T(8,128)(2,1)S(1)} %get-tuple-element.149.refs_2_), channel_id=1, source_target_pairs={{0,8},{2,10},{4,12},{6,14},{8,0},{10,2},{12,4},{14,6},{16,24},{18,... | collective-permute-start | bytes 884744 | tf_op jit(solution)/shard_map/cond/branch_1_fun/ppermute | solution.py:497
  226.7 37.8 %collective-permute-start.14 = (bf16[512,512]{1,0:T(8,128)(2,1)}, bf16[512,512]{1,0:T(8,128)(2,1)}, u32[]{:S(2)}, u32[]{:S(2)}) collective-permute-start(bf16[512,512]{1,0:T(8,128)(2,1)} %get-tuple-element.426), channel_id=1, source_target_pairs={{0,2},{2,0},{4,6},{6,4},{8,10},{10,8},{12,14},{14,12},{16,18},{18,... | collective-permute-start | bytes 1572872 | tf_op jit(solution)/shard_map/cond/branch_1_fun/ppermute | solution.py:497
  228.2 36.4 %collective-permute-start.15 = (bf16[512,512]{1,0:T(8,128)(2,1)}, bf16[512,512]{1,0:T(8,128)(2,1)}, u32[]{:S(2)}, u32[]{:S(2)}) collective-permute-start(bf16[512,512]{1,0:T(8,128)(2,1)} %get-tuple-element.426), channel_id=1, source_target_pairs={{0,4},{2,6},{4,0},{6,2},{8,12},{10,14},{12,8},{14,10},{16,20},{18,... | collective-permute-start | bytes 1572872 | tf_op jit(solution)/shard_map/cond/branch_1_fun/ppermute | solution.py:497
  228.6 33.0 %collective-permute-start.18 = (bf16[288,512]{1,0:T(8,128)(2,1)S(1)}, bf16[288,512]{1,0:T(8,128)(2,1)S(1)}, u32[]{:S(2)}, u32[]{:S(2)}) collective-permute-start(bf16[288,512]{1,0:T(8,128)(2,1)S(1)} %get-tuple-element.156.refs_0_), channel_id=1, source_target_pairs={{0,16},{2,18},{4,20},{6,22},{8,24},{10,26},{12,28},{14,30},{16,0},... | collective-permute-start | bytes 884744 | tf_op jit(solution)/shard_map/cond/branch_1_fun/ppermute | solution.py:497
  262.9 10.3 %collective-permute-start.19 = (bf16[288,512]{1,0:T(8,128)(2,1)}, bf16[288,512]{1,0:T(8,128)(2,1)}, u32[]{:S(2)}, u32[]{:S(2)}) collective-permute-start(bf16[288,512]{1,0:T(8,128)(2,1)} %reduce_step.11), channel_id=1, source_target_pairs={{0,2},{2,0},{4,6},{6,4},{8,10},{10,8},{12,14},{14,12},{16,18},{18,... | collective-permute-start | bytes 884744 | tf_op jit(solution)/shard_map/cond/branch_1_fun/ppermute | solution.py:497
  263.0 10.3 %collective-permute-start.20 = (bf16[288,512]{1,0:T(8,128)(2,1)}, bf16[288,512]{1,0:T(8,128)(2,1)}, u32[]{:S(2)}, u32[]{:S(2)}) collective-permute-start(bf16[288,512]{1,0:T(8,128)(2,1)} %reduce_step.11), channel_id=1, source_target_pairs={{0,4},{2,6},{4,0},{6,2},{8,12},{10,14},{12,8},{14,10},{16,20},{18,... | collective-permute-start | bytes 884744 | tf_op jit(solution)/shard_map/cond/branch_1_fun/ppermute | solution.py:497
  265.5 16.5 %collective-permute-start.16 = (bf16[256,512]{1,0:T(8,128)(2,1)S(1)}, bf16[256,512]{1,0:T(8,128)(2,1)}, u32[]{:S(2)}, u32[]{:S(2)}) collective-permute-start(bf16[256,512]{1,0:T(8,128)(2,1)S(1)} %slice.46), channel_id=1, source_target_pairs={{0,4},{2,6},{4,0},{6,2},{8,12},{10,14},{12,8},{14,10},{16,20},{18,... | collective-permute-start | bytes 786440 | tf_op jit(solution)/shard_map/cond/branch_1_fun/ppermute | solution.py:497
  267.1 14.9 %collective-permute-start.17 = (bf16[256,512]{1,0:T(8,128)(2,1)S(1)}, bf16[256,512]{1,0:T(8,128)(2,1)}, u32[]{:S(2)}, u32[]{:S(2)}) collective-permute-start(bf16[256,512]{1,0:T(8,128)(2,1)S(1)} %slice.47), channel_id=1, source_target_pairs={{0,2},{2,0},{4,6},{6,4},{8,10},{10,8},{12,14},{14,12},{16,18},{18,... | collective-permute-start | bytes 786440 | tf_op jit(solution)/shard_map/cond/branch_1_fun/ppermute | solution.py:497
  (53 other events, 334.5 us)
Sparse Core Ops, SparseCore 0:
  93.4 174.7 all-reduce.8
